TPU v7x, 32 devices: a whole 2x2x4 slice. The times are simulated.
32 devices in a mesh: groups: 2 (over y), view: 4 (over z), col: 4 (over x, core).
Axes of the slice: x: 2, y: 2, z: 4, core: 2. Of those that a mesh axis runs over, the one named last changes fastest.
Arguments:
- volume: bfloat16 [2048, 512], P(('groups', 'view'), 'col'), parts along dimension 0, may hold values from -6 to 6
- requests: int32 [8, 4, 16], P(('groups', 'view')), parts along dimension 0, may hold values from 0 to 255, as said below
- counts: int32 [8, 4], P(('groups', 'view')), parts along dimension 0, may hold values from 1 to 16, as said below
- axial: bfloat16 [128, 4, 64], P('view'), may hold values from -0.75 to 0.75
- footprint: bfloat16 [128, 128, 1024], P('view', None, 'col'), may hold values from -0.5 to 0.5
- dual: bfloat16 [256, 4, 1024], P(('groups', 'view'), None, 'col'), parts along dimension 0, may hold values from -6 to 6
- measured: bfloat16 [256, 4, 1024], P(('groups', 'view'), None, 'col'), parts along dimension 0, may hold values from -6 to 6
- conv_first: bfloat16 [3, 3, 32, 3], replicated, may hold values from -1.25 to 1.25
- slopes_first: float32 [32], replicated, may hold values from 0.05 to 0.5
- conv_second: bfloat16 [3, 3, 32, 32], replicated, may hold values from -0.375 to 0.375
- slopes_second: float32 [32], replicated, may hold values from 0.05 to 0.5
- conv_last: bfloat16 [3, 3, 1, 32], replicated, may hold values from -0.375 to 0.375
Outputs:
- dual_out: bfloat16 [256, 4, 1024], P(('groups', 'view'), None, 'col'), parts along dimension 0
- backprojection: float32 [2048, 512], P(('groups', 'view'), 'col'), parts along dimension 0
There are 2 independent parts, one for each index of `groups`. A program takes and returns all parts, laid end to end along the dimension named above; an argument that names none is the same for every part. Nothing has to cross between parts.
Inputs may be any that keep to these rules, and one draw needn't show every extreme that they name: Entry requests[o, g, s] names tile o * 256 + requests[o, g, s]; for each o and g the first counts[o, g] entries are distinct and the others are not used. `counts`: in every draw one view group takes 16 tiles from every owner.
All inputs are finite; a program needn't handle non-finite values.
Results may differ from a plain program's by a relative error of at most 0.0054.
Values may be sent and summed in bfloat16 or wider, within the bound.
No kernel may reach another device: no remote copies, remote signals or barrier semaphores. Data moves between devices by JAX's collectives and lax.ppermute only.
A program may use at most 128 MiB of HBM per device.

v0:
```python
import functools

import jax
import jax.numpy as jnp
import numpy as np
from jax import lax
from jax.experimental import pallas as pl
from jax.experimental.pallas import tpu as pltpu
from jax.sharding import PartitionSpec as P

HALO = 3
BAND = 8
STEP = 6
LANES = 128
EDGE_ROWS = 16
VM = pl.BlockSpec(memory_space=pltpu.VMEM)
SM = pl.BlockSpec(memory_space=pltpu.SMEM)
F32 = jnp.float32
BF16 = jnp.bfloat16


def call(body, outs, scratch, args, specs=None, cost=None):
    single = not isinstance(outs, (list, tuple))
    return pl.pallas_call(
        body,
        out_shape=outs if single else list(outs),
        in_specs=specs or [VM] * len(args),
        out_specs=VM if single else [VM] * len(outs),
        scratch_shapes=scratch,
        compiler_params=pltpu.CompilerParams(vmem_limit_bytes=40 * 1024 * 1024),
        cost_estimate=cost and pl.CostEstimate(flops=cost[0], bytes_accessed=cost[1], transcendentals=0),
    )(*args)


def shape(dims, dtype=F32):
    return jax.ShapeDtypeStruct(dims, dtype)


def swap_perms(n):
    first = [(i, i ^ 1) for i in range(n)]
    second = [(i, (i + 1) % n if i % 2 else (i - 1) % n) for i in range(n)]
    return first, second


def both_ways(array_a, array_b, axis):
    first, second = swap_perms(lax.axis_size(axis))
    return lax.ppermute(array_a, axis, first), lax.ppermute(array_b, axis, second)


def exchange(pieces, axis):
    n = lax.axis_size(axis)
    if len(pieces) == 1:
        return [lax.all_to_all(pieces[0], axis, split_axis=0, concat_axis=0, tiled=True)]
    return [pieces[0]] + [lax.ppermute(pieces[k], axis, [(i, i ^ k) for i in range(n)]) for k in range(1, n)]


def gather_kernel(n, slots, split, req_ref, cnt_ref, vol_ref, *rest):
    outs, (vol_s, out_s) = rest[:-2], rest[-2:]
    tiles = vol_ref.shape[0]
    vol_s[0:tiles, :] = vol_ref[...].astype(F32)
    vol_s[tiles : tiles + 8, :] = jnp.zeros((8, vol_ref.shape[1]), F32)
    me = lax.axis_index("view")

    def chunk(k, dest):
        count = cnt_ref[0, dest]
        for s in range(slots):
            row = jnp.where(s < count, req_ref[0, dest, s], tiles)
            out_s[pl.ds(k * slots + s, 1), :] = vol_s[pl.ds(row, 1), :]

    if split:
        for k in range(n):
            chunk(k, me ^ k)
            outs[k][...] = out_s[k * slots : (k + 1) * slots, :].astype(BF16)
    else:
        lax.fori_loop(0, n, lambda k, c: (chunk(k, k), c)[1], 0)
        outs[0][...] = out_s[...].astype(BF16)


def scatter_kernel(n, slots, split, req_ref, cnt_ref, *rest):
    pieces, out_ref, acc = rest[:-2], rest[-2], rest[-1]
    tiles = out_ref.shape[0]
    acc[...] = jnp.zeros(acc.shape, F32)
    me = lax.axis_index("view")

    def chunk(source, dest):
        count = cnt_ref[0, dest]
        rows = [jnp.where(s < count, req_ref[0, dest, s], tiles) for s in range(slots)]
        sums = [acc[pl.ds(rows[s], 1), :] + source(s) for s in range(slots)]
        for s in range(slots):
            acc[pl.ds(rows[s], 1), :] = sums[s]

    if split:
        for k in range(n):
            chunk(lambda s: pieces[k][s : s + 1, :], me ^ k)
    else:
        lax.fori_loop(0, n, lambda k, c: (chunk(lambda s: pieces[0][pl.ds(k * slots + s, 1), :], k), c)[1], 0)
    out_ref[...] = acc[0:tiles, :]


def put_flat(flat_ref, start, block):
    for t in range(flat_ref.shape[0]):
        flat_ref[t, start : start + block.shape[0], :] = block[:, t * LANES : (t + 1) * LANES]


def widen(flat_ref, rows):
    tiles, both, _ = flat_ref.shape
    return jnp.concatenate(
        [flat_ref[t, pl.ds(r, both // rows, stride=rows), :] for r in range(rows) for t in range(tiles)], axis=1
    )


def widen_kernel(dual_ref, meas_ref, out_ref, flat):
    views, rows, _ = dual_ref.shape
    for i, ref in enumerate((dual_ref, meas_ref)):
        for v in range(views):
            put_flat(flat, v * rows, ref[v].astype(F32))
        out_ref[i] = widen(flat, rows)


def forward_kernel(n, rows, axial_ref, foot_ref, stat_ref, *rest):
    pieces, (fw_ref, a_ref, b_ref, slots_s, flat, edge) = rest[:-6], rest[-6:]
    me = lax.axis_index("view")
    views = foot_ref.shape[0]
    if len(pieces) > 1:
        cap = pieces[0].shape[0]
        for k in range(n):
            slots_s[pl.ds(pl.multiple_of((me ^ k) * cap, cap), cap), :] = pieces[k][...]
        slot_rows = slots_s[...]
    else:
        slot_rows = pieces[0][...]
    axial_sum = jnp.dot(axial_ref[...], slot_rows, preferred_element_type=F32).astype(BF16)
    per = 16 // rows
    owner = lax.broadcasted_iota(jnp.int32, (16, foot_ref.shape[2]), 0) // rows
    for q in range(views // per):
        lhs = axial_sum[16 * q : 16 * q + 16, :]
        got = None
        for i in range(per):
            one = jnp.dot(lhs, foot_ref[q * per + i], preferred_element_type=F32)
            got = one if got is None else jnp.where(owner == i, one, got)
        put_flat(flat, 16 * q, got.astype(BF16).astype(F32))
    fw = widen(flat, rows)
    fw_ref[...] = fw
    edge[...] = jnp.zeros(edge.shape, F32)
    for way, start in ((0, 0), (1, views - HALO)):
        for c in range(3):
            part = fw[start : start + HALO, :] if c == 1 else stat_ref[c // 2, start : start + HALO, :]
            edge[way, c * HALO : (c + 1) * HALO, :] = part
    even = me % 2 == 0
    to_prev, to_next = edge[0], edge[1]
    a_ref[...] = jnp.where(even, to_next, to_prev).astype(BF16)
    b_ref[...] = jnp.where(even, to_prev, to_next).astype(BF16)


def halo_of(a_ref, b_ref, channel):
    even = lax.axis_index("view") % 2 == 0
    rows = slice(channel * HALO, (channel + 1) * HALO)
    a = a_ref[...].astype(F32)[rows]
    b = b_ref[...].astype(F32)[rows]
    return jnp.where(even, b, a), jnp.where(even, a, b)


def lane(shape_):
    return lax.broadcasted_iota(jnp.int32, shape_, 1)


def strip_of(wide, rows, inner):
    cols = wide.shape[1] // rows
    at = lane((wide.shape[0], LANES))
    total = jnp.zeros((wide.shape[0], LANES), F32)
    for r in range(rows):
        head = wide[:, r * cols : r * cols + LANES]
        tail = wide[:, (r + 1) * cols - LANES : (r + 1) * cols]
        left, right = 16 * r, 64 + 16 * r
        if inner:
            picks = ((head, 0, left + HALO, 6), (tail, LANES - 6, right, 6))
        else:
            picks = ((tail, LANES - HALO, left, HALO), (head, 0, right + 6, HALO))
        for source, begin, target, width in picks:
            moved = pltpu.roll(source, (target - begin) % LANES, 1)
            total = jnp.where((at >= target) & (at < target + width), moved, total)
    return total


def own_strip_kernel(rows, fw_ref, stat_ref, in_ref, msg_ref):
    for c in range(3):
        wide = fw_ref[...] if c == 1 else stat_ref[c // 2]
        in_ref[c] = strip_of(wide, rows, True)
        msg_ref[c] = strip_of(wide, rows, False)


def strip_message_kernel(rows, in_ref, msg_ref, a_ref, b_ref, strip_ref, out_ref, buf):
    views = in_ref.shape[1]
    buf[...] = jnp.zeros(buf.shape, F32)
    strip_ref[...] = jnp.zeros(strip_ref.shape, F32)
    for c in range(3):
        for start, part in zip((0, HALO + views), halo_of(a_ref, b_ref, c)):
            strip_ref[c, start : start + HALO, :] = strip_of(part, rows, True)
            buf[c, start : start + HALO, :] = strip_of(part, rows, False)
        strip_ref[c, HALO : HALO + views, :] = in_ref[c]
        buf[c, HALO : HALO + views, :] = msg_ref[c]
        out_ref[c] = buf[c].astype(BF16)


def prelu(z, slopes_ref):
    channels = slopes_ref.shape[0]
    slopes = jnp.concatenate([slopes_ref[...]] * (z.shape[0] // channels), axis=0)
    slopes = jnp.concatenate([slopes] * (z.shape[1] // LANES), axis=1)
    return jnp.maximum(z, slopes * z)


def network(inputs, views, w1, w2, w3, a1, a2, s1, s2, s3, update, inside=None):
    n = s2.shape[2]
    channels = a1.shape[0]
    for c in range(3):
        x = inputs(c)
        s1[c] = pltpu.roll(x, 1, 1)
        s1[3 + c] = x
        s1[6 + c] = pltpu.roll(x, n - 1, 1)
    total = views + 4
    for k in range(-(-total // BAND)):
        m = min(BAND, total - BAND * k) * channels
        window = jnp.concatenate([s1[j, BAND * k : BAND * k + 16, :] for j in range(9)], axis=0).astype(BF16)
        z = prelu(jnp.dot(w1[0:m, :], window, preferred_element_type=F32), a1)
        if inside is not None:
            z = jnp.where(inside, z, 0.0)
        at = slice(BAND * k * channels, BAND * k * channels + m)
        s2[0, at, :] = pltpu.roll(z, 1, 1).astype(BF16)
        s2[1, at, :] = z.astype(BF16)
        s2[2, at, :] = pltpu.roll(z, n - 1, 1).astype(BF16)
    total = views + 2
    for k in range(-(-total // STEP)):
        count = min(STEP, total - STEP * k)
        m, depth = count * channels, (count + 2) * channels
        begin = STEP * k * channels
        if count == STEP:
            window = jnp.concatenate([s2[b, begin : begin + depth, :] for b in range(3)], axis=0)
            z = jnp.dot(w2[...], window, preferred_element_type=F32)
        else:
            full = (STEP + 2) * channels
            z = sum(
                jnp.dot(w2[0:m, b * full : b * full + depth], s2[b, begin : begin + depth, :], preferred_element_type=F32)
                for b in range(3)
            )
        z = prelu(z, a2)
        if inside is not None:
            z = jnp.where(inside, z, 0.0)
        s3[begin : begin + m, :] = z.astype(BF16)
    for k in range(-(-views // STEP)):
        count = min(STEP, views - STEP * k)
        depth = (count + 2) * channels
        begin = STEP * k * channels
        got = jnp.dot(w3[:, 0:depth], s3[begin : begin + depth, :], preferred_element_type=F32)
        out = pltpu.roll(got[0:8], 1, 1) + got[8:16] + pltpu.roll(got[16:24], n - 1, 1)
        update[STEP * k : STEP * k + count, :] = out[0:count, :]


def main_kernel(rows, fw_ref, stat_ref, ha_ref, hb_ref, w1, w2, w3, a1, a2, out_ref, x, s1, s2, s3, update):
    views = fw_ref.shape[0]
    x[...] = jnp.zeros(x.shape, F32)
    for c in range(3):
        before, after = halo_of(ha_ref, hb_ref, c)
        x[c, 0:HALO, :] = before
        x[c, HALO : HALO + views, :] = fw_ref[...] if c == 1 else stat_ref[c // 2]
        x[c, HALO + views : 2 * HALO + views, :] = after
    cols = fw_ref.shape[1] // rows
    for r in range(rows):
        at = slice(r * cols, (r + 1) * cols)
        network(lambda c: x[c, :, at], views, w1, w2, w3, a1, a2, s1, s2, s3, update)
        out_ref[:, at] = stat_ref[0, :, at] + update[...]


def back_kernel(
    n, rows, strip_ref, ra_ref, rb_ref, w1, w2, w3, a1, a2, main_ref, foot_ref, axial_ref, dual_ref, *rest
):
    parts, (x, s1, s2, s3, update, flat, back, part_s) = rest[:-8], rest[-8:]
    views, _, cols = foot_ref.shape[0], foot_ref.shape[1], foot_ref.shape[2]
    me, peers = lax.axis_index("col"), lax.axis_size("col")
    even = me % 2 == 0
    at = lane((1, LANES))
    left_side, step = at < 64, at % 16
    from_left = left_side & (step < HALO) & (me > 0)
    from_right = (~left_side) & (step >= 6) & (step < 9) & (me < peers - 1)
    inside = (left_side & ((step >= HALO) | (me > 0))) | ((~left_side) & ((step < 6) | (me < peers - 1)))
    for c in range(3):
        a, b = ra_ref[c].astype(F32), rb_ref[c].astype(F32)
        right = jnp.where(even, a, b)
        left = jnp.where(even, b, a)
        x[c] = jnp.where(from_left, left, jnp.where(from_right, right, strip_ref[c]))
    network(lambda c: x[c], views, w1, w2, w3, a1, a2, s1, s2, s3, update, inside)
    strip = x[0, HALO : HALO + views, :] + update[...]
    first = lane((views, LANES))
    for r in range(rows):
        head = main_ref[:, r * cols : r * cols + LANES]
        tail = main_ref[:, (r + 1) * cols - LANES : (r + 1) * cols]
        moved = pltpu.roll(strip, (-(16 * r + HALO)) % LANES, 1)
        head = jnp.where(first < HALO, moved, head)
        moved = pltpu.roll(strip, (LANES - HALO - (64 + 16 * r + HALO)) % LANES, 1)
        tail = jnp.where(first >= LANES - HALO, moved, tail)
        for t in range(cols // LANES):
            middle = main_ref[:, r * cols + t * LANES : r * cols + (t + 1) * LANES]
            last = cols // LANES - 1
            flat[t, pl.ds(r, views, stride=rows), :] = head if t == 0 else tail if t == last else middle
    per = 16 // rows
    owner = lax.broadcasted_iota(jnp.int32, (16, foot_ref.shape[1]), 0) // rows
    for q in range(views // per):
        block = jnp.concatenate([flat[t, 16 * q : 16 * q + 16, :] for t in range(cols // LANES)], axis=1).astype(BF16)
        dual_ref[16 * q : 16 * q + 16, :] = block
        got = None
        for i in range(per):
            one = lax.dot_general(
                block, foot_ref[q * per + i], (((1,), (1,)), ((), ())), preferred_element_type=F32
            )
            got = one if got is None else jnp.where(owner == i, one, got)
        back[16 * q : 16 * q + 16, :] = got.astype(BF16)
    partial = jnp.dot(axial_ref[...], back[...], preferred_element_type=F32)
    if len(parts) > 1:
        part_s[...] = partial
        cap = parts[0].shape[0]
        group = lax.axis_index("view")
        for k in range(n):
            parts[k][...] = part_s[pl.ds(pl.multiple_of((group ^ k) * cap, cap), cap), :]
    else:
        parts[0][...] = partial


def banded_weights(conv_first, conv_second, conv_last):
    channels = conv_second.shape[3]
    move = np.zeros((BAND, 3, 3, 3, 3, 3, 16), np.float32)
    for v in range(BAND):
        for a in range(3):
            for b in range(3):
                for c in range(3):
                    move[v, b, c, a, b, c, v + a] = 1.0
    move = jnp.asarray(move.reshape(BAND, 27, 144), BF16)
    first = conv_first.transpose(2, 1, 3, 0).reshape(channels, 27)
    w1 = jnp.einsum("ok,vkn->von", first, move, preferred_element_type=F32).astype(BF16)
    w1 = w1.reshape(BAND * channels, 144)

    def slide(w, steps):
        return jnp.stack(
            [
                jnp.pad(w, [(0, 0)] * (w.ndim - 1) + [(v * channels, (STEP - 1 - v) * channels)])
                for v in range(steps)
            ]
        )

    second = conv_second.transpose(1, 2, 0, 3).reshape(3, channels, 3 * channels)
    w2 = slide(second, STEP).transpose(0, 2, 1, 3).reshape(STEP * channels, 3 * (STEP + 2) * channels)
    last = conv_last.transpose(1, 2, 0, 3).reshape(3, 3 * channels)
    w3 = slide(last, STEP).transpose(1, 0, 2)
    w3 = jnp.pad(w3, ((0, 0), (0, 8 - STEP), (0, 0))).reshape(24, (STEP + 2) * channels)
    return w1, w2, w3


def shards(
    volume,
    requests,
    counts,
    axial,
    footprint,
    dual,
    measured,
    conv_first,
    slopes_first,
    conv_second,
    slopes_second,
    conv_last,
):
    n = lax.axis_size("view")
    slots = requests.shape[2]
    tiles, vox = volume.shape
    views, rows, cols = dual.shape
    wide = rows * cols
    channels = conv_second.shape[2]
    split = n in (2, 4)
    pieces = [shape((slots, vox), BF16)] * n if split else [shape((n * slots, vox), BF16)]
    outgoing = call(
        functools.partial(gather_kernel, n, slots, split),
        pieces,
        [pltpu.VMEM((tiles + 8, vox), F32), pltpu.VMEM((n * slots, vox), F32)],
        [requests, counts, volume],
        [SM, SM, VM],
    )
    incoming = exchange(outgoing, "view")

    stat = call(widen_kernel, shape((2, views, wide)), [pltpu.VMEM((cols // LANES, views * rows, LANES), F32)], [dual, measured])
    w1, w2, w3 = banded_weights(conv_first, conv_second, conv_last)
    a1 = jnp.broadcast_to(slopes_first[:, None], (channels, LANES))
    a2 = jnp.broadcast_to(slopes_second[:, None], (channels, LANES))
    axial_flat = axial.reshape(views * rows, n * slots)
    axial_back = axial_flat.T

    edge = shape((EDGE_ROWS, wide), BF16)
    fw, edge_a, edge_b = call(
        functools.partial(forward_kernel, n, rows),
        [shape((views, wide)), edge, edge],
        [
            pltpu.VMEM((n * slots, vox), BF16),
            pltpu.VMEM((cols // LANES, views * rows, LANES), F32),
            pltpu.VMEM((2, EDGE_ROWS, wide), F32),
        ],
        [axial_flat, footprint, stat, *incoming],
    )
    halo_a, halo_b = both_ways(edge_a, edge_b, "view")
    own = shape((3, views, LANES))
    strip_in, strip_msg = call(functools.partial(own_strip_kernel, rows), [own, own], [], [fw, stat])
    padded = 48
    strip, message = call(
        functools.partial(strip_message_kernel, rows),
        [shape((3, padded, LANES)), shape((3, padded, LANES), BF16)],
        [pltpu.VMEM((3, padded, LANES), F32)],
        [strip_in, strip_msg, halo_a, halo_b],
    )
    side_a, side_b = both_ways(message, message, "col")

    def net_scratch(width):
        return [
            pltpu.VMEM((9, padded, width), F32),
            pltpu.VMEM((3, (views + 4) * channels, width), BF16),
            pltpu.VMEM(((views + 2) * channels, width), BF16),
            pltpu.VMEM((views, width), F32),
        ]

    main = call(
        functools.partial(main_kernel, rows),
        shape((views, wide)),
        [pltpu.VMEM((3, padded, wide), F32), *net_scratch(cols)],
        [fw, stat, halo_a, halo_b, w1, w2, w3, a1, a2],
        cost=(2 * 10**9, 4 * 10**6),
    )
    parts = [shape((slots, vox))] * n if split else [shape((n * slots, vox))]
    dual_out, *returned = call(
        functools.partial(back_kernel, n, rows),
        [shape((views * rows, cols), BF16), *parts],
        [
            pltpu.VMEM((3, padded, LANES), F32),
            *net_scratch(LANES),
            pltpu.VMEM((cols // LANES, views * rows, LANES), F32),
            pltpu.VMEM((views * rows, vox), BF16),
            pltpu.VMEM((n * slots, vox), F32),
        ],
        [strip, side_a, side_b, w1, w2, w3, a1, a2, main, footprint, axial_back],
    )
    arrived = exchange(returned, "view")
    backprojection = call(
        functools.partial(scatter_kernel, n, slots, split),
        shape((tiles, vox)),
        [pltpu.VMEM((tiles + 8, vox), F32)],
        [requests, counts, *arrived],
        [SM, SM] + [VM] * len(arrived),
    )
    return dual_out.reshape(views, rows, cols), backprojection


def solution(mesh):
    in_specs = (
        P(("groups", "view"), "col"),
        P(("groups", "view"), None, None),
        P(("groups", "view"), None),
        P("view", None, None),
        P("view", None, "col"),
        P(("groups", "view"), None, "col"),
        P(("groups", "view"), None, "col"),
        P(),
        P(),
        P(),
        P(),
        P(),
    )
    out_specs = (P(("groups", "view"), None, "col"), P(("groups", "view"), "col"))
    return jax.shard_map(shards, mesh=mesh, in_specs=in_specs, out_specs=out_specs, check_vma=False)
```

profile of v0, /device:TPU:0, one launch (start us, length us, event | category | flops | bytes accessed | tf_op | source)
XLA Modules:
  0.0 43.3 jit_solution(9932817014042412856)
XLA Ops:
  0.7 0.8 %copy-done.4 = bf16[256,128]{1,0:T(8,128)(2,1)S(1)} copy-done((bf16[256,128]{1,0:T(8,128)(2,1)S(1)}, bf16[256,128]{1,0:T(8,128)(2,1)}, u32[]{:S(2)}) %copy-start.4) | copy-done | bytes 65560
  1.5 0.7 %copy-done.7 = s32[1,4,16]{2,1,0:T(4,128)S(1)} copy-done((s32[1,4,16]{2,1,0:T(4,128)S(1)}, s32[1,4,16]{2,1,0:T(4,128)}, u32[]{:S(2)}) %copy-start.7) | copy-done | bytes 280
  2.2 0.7 %copy-done.9 = s32[1,4]{1,0:T(1,128)S(1)} copy-done((s32[1,4]{1,0:T(1,128)S(1)}, s32[1,4]{1,0:T(1,128)}, u32[]{:S(2)}) %copy-start.9) | copy-done | bytes 40
  2.8 0.7 %shard_map.141 = (bf16[16,128]{1,0:T(8,128)(2,1)S(1)}, bf16[16,128]{1,0:T(8,128)(2,1)S(1)}, bf16[16,128]{1,0:T(8,128)(2,1)S(1)}, bf16[16,128]{1,0:T(8,128)(2,1)S(1)}) custom-call(s32[1,4,16]{2,1,0:T(4,128)S(1)} %copy-done.7, s32[1,4]{1,0:T(1,128)S(1)} %copy-done.9, bf16[256,128]{1,0:T(8,128)(2,1)S(1)} %copy-done.4), custom_call_target="tpu_custom_call" | custom-call | tf_op jit(solution)/shard_map/pallas_call | solution.py:24
  3.5 3.1 %collective-permute-start = (bf16[16,128]{1,0:T(8,128)(2,1)S(1)}, bf16[16,128]{1,0:T(8,128)(2,1)S(1)}, u32[]{:S(2)}, u32[]{:S(2)}) collective-permute-start(bf16[16,128]{1,0:T(8,128)(2,1)S(1)} %get-tuple-element.19), channel_id=1, source_target_pairs={{0,4},{4,0},{8,12},{12,8},{1,5},{5,1},{9,13},{13,9},{2,6},{6,2},{1... | collective-permute-start | bytes 12296 | tf_op jit(solution)/shard_map/ppermute | solution.py:54
  6.6 2.6 %collective-permute-start.1 = (bf16[16,128]{1,0:T(8,128)(2,1)S(1)}, bf16[16,128]{1,0:T(8,128)(2,1)S(1)}, u32[]{:S(2)}, u32[]{:S(2)}) collective-permute-start(bf16[16,128]{1,0:T(8,128)(2,1)S(1)} %get-tuple-element.20), channel_id=1, source_target_pairs={{0,8},{4,12},{8,0},{12,4},{1,9},{5,13},{9,1},{13,5},{2,10},{6,14},... | collective-permute-start | bytes 12296 | tf_op jit(solution)/shard_map/ppermute | solution.py:54
  9.2 0.9 %copy.24 = bf16[3,32,3,32]{3,2,1,0:T(4,128)(2,1)S(1)} copy(bf16[3,32,3,32]{3,1,0,2:T(8,128)(2,1)} %bitcast.56) | data formatting | bytes 36864 | tf_op jit(solution)/shard_map/transpose | solution.py:347
  10.6 0.7 %copy.26 = bf16[3,1,3,32]{3,2,0,1:T(4,128)(2,1)S(1)} copy(bf16[3,1,3,32]{3,0,1,2:T(4,128)(2,1)} %bitcast.59) | data formatting | bytes 1152 | tf_op jit(solution)/shard_map/transpose | solution.py:349
  11.7 0.7 %copy.22 = bf16[32,3,3,3]{0,3,2,1:T(4,128)(2,1)S(1)} copy(bf16[32,3,3,3]{0,2,1,3:T(4,128)(2,1)} %bitcast.58) | data formatting | bytes 3456 | tf_op jit(solution)/shard_map/transpose | solution.py:335
  12.4 1.1 %convolution_convert_fusion = bf16[8,144,32]{1,2,0:T(8,128)(2,1)S(1)} fusion(bf16[8,27,144]{2,1,0:T(8,128)(2,1)} %constant.5.clone, bf16[32,27]{0,1:T(8,128)(2,1)S(1)} %reshape.31), kind=kOutput, calls=%fused_computation | convolution fusion | flops 2027520 | bytes 137664 | tf_op jit(solution)/shard_map/ok,vkn->von/dot_general | solution.py:336
  13.6 0.8 %copy-done.5 = bf16[32,4,256]{2,1,0:T(4,128)(2,1)S(1)} copy-done((bf16[32,4,256]{2,1,0:T(4,128)(2,1)S(1)}, bf16[32,4,256]{2,1,0:T(4,128)(2,1)}, u32[]{:S(2)}) %copy-start.5) | copy-done | bytes 65560
  14.5 0.8 %copy-done.6 = bf16[32,4,256]{2,1,0:T(4,128)(2,1)S(1)} copy-done((bf16[32,4,256]{2,1,0:T(4,128)(2,1)S(1)}, bf16[32,4,256]{2,1,0:T(4,128)(2,1)}, u32[]{:S(2)}) %copy-start.6) | copy-done | bytes 65560
  15.4 1.6 %copy-done = bf16[32,128,256]{2,1,0:T(8,128)(2,1)S(1)} copy-done((bf16[32,128,256]{2,1,0:T(8,128)(2,1)S(1)}, bf16[32,128,256]{2,1,0:T(8,128)(2,1)}, u32[]{:S(2)}) %copy-start) | copy-done | bytes 2097176
  17.0 0.8 %copy-done.2 = bf16[32,4,64]{2,1,0:T(4,128)(2,1)S(1)} copy-done((bf16[32,4,64]{2,1,0:T(4,128)(2,1)S(1)}, bf16[32,4,64]{2,1,0:T(4,128)(2,1)}, u32[]{:S(2)}) %copy-start.2) | copy-done | bytes 16408
  18.3 1.0 %collective-permute-start.3 = (bf16[16,1024]{1,0:T(8,128)(2,1)S(1)}, bf16[16,1024]{1,0:T(8,128)(2,1)S(1)}, u32[]{:S(2)}, u32[]{:S(2)}) collective-permute-start(bf16[16,1024]{1,0:T(8,128)(2,1)S(1)} %get-tuple-element.25), channel_id=1, source_target_pairs={{0,4},{4,0},{8,12},{12,8},{1,5},{5,1},{9,13},{13,9},{2,6},{6,2},{1... | collective-permute-start | bytes 98312 | tf_op jit(solution)/shard_map/ppermute | solution.py:47
  19.2 3.0 %collective-permute-start.4 = (bf16[16,1024]{1,0:T(8,128)(2,1)S(1)}, bf16[16,1024]{1,0:T(8,128)(2,1)S(1)}, u32[]{:S(2)}, u32[]{:S(2)}) collective-permute-start(bf16[16,1024]{1,0:T(8,128)(2,1)S(1)} %get-tuple-element.26), channel_id=1, source_target_pairs={{0,12},{4,8},{8,4},{12,0},{1,13},{5,9},{9,5},{13,1},{2,14},{6,10},... | collective-permute-start | bytes 98312 | tf_op jit(solution)/shard_map/ppermute | solution.py:47
  23.0 2.0 %collective-permute-done.4.b_ref.hb_ref = bf16[16,1024]{1,0:T(8,128)(2,1)S(1)} collective-permute-done((bf16[16,1024]{1,0:T(8,128)(2,1)S(1)}, bf16[16,1024]{1,0:T(8,128)(2,1)S(1)}, u32[]{:S(2)}, u32[]{:S(2)}) %collective-permute-start.4) | collective-permute-done | bytes 32800 | tf_op jit(solution)/shard_map/ppermute | solution.py:47
  25.2 1.6 %collective-permute-start.6 = (bf16[3,48,128]{2,1,0:T(8,128)(2,1)S(1)}, bf16[3,48,128]{2,1,0:T(8,128)(2,1)S(1)}, u32[]{:S(2)}, u32[]{:S(2)}) collective-permute-start(bf16[3,48,128]{2,1,0:T(8,128)(2,1)S(1)} %get-tuple-element.28), channel_id=1, source_target_pairs={{0,3},{1,2},{2,1},{3,0},{4,7},{5,6},{6,5},{7,4},{8,11},{9,10},{10,... | collective-permute-start | bytes 110600 | tf_op jit(solution)/shard_map/ppermute | solution.py:47
  26.9 4.0 %shard_map.145.main_ref = f32[32,1024]{1,0:T(8,128)S(1)} custom-call(f32[32,1024]{1,0:T(8,128)S(1)} %get-tuple-element.22.fw_ref, f32[2,32,1024]{2,1,0:T(8,128)S(1)} %shard_map.140.stat_ref, bf16[16,1024]{1,0:T(8,128)(2,1)S(1)} %collective-permute-done.3.a_ref.ha_ref, bf16[16,1024]{1,0:T(8,128)(2,1)S(1)} %collective-permute-done.4.b_ref.hb_ref, ...), custom_call_target="tpu_custom_call" | custom-call | flops 2000000000 | bytes 4000000 | tf_op jit(solution)/shard_map/pallas_call | solution.py:24
  31.0 1.9 %shard_map.146 = (bf16[128,256]{1,0:T(8,128)(2,1)S(1)}, f32[16,128]{1,0:T(8,128)S(1)}, f32[16,128]{1,0:T(8,128)S(1)}, f32[16,128]{1,0:T(8,128)S(1)}, f32[16,128]{1,0:T(8,128)S(1)}) custom-call(f32[3,48,128]{2,1,0:T(8,128)S(1)} %get-tuple-element.27.strip_ref, bf16[3,48,128]{2,1,0:T(8,128)(2,1)S(1)} %collective-permute-done.5.ra_ref, ...), custom_call_target="tpu_custom_call" | custom-call | tf_op jit(solution)/shard_map/pallas_call | solution.py:24
  33.1 3.3 %collective-permute-start.8 = (f32[16,128]{1,0:T(8,128)S(1)}, f32[16,128]{1,0:T(8,128)S(1)}, u32[]{:S(2)}, u32[]{:S(2)}) collective-permute-start(f32[16,128]{1,0:T(8,128)S(1)} %get-tuple-element.32), channel_id=1, source_target_pairs={{0,8},{4,12},{8,0},{12,4},{1,9},{5,13},{9,1},{13,5},{2,10},{6,14},... | collective-permute-start | bytes 24584 | tf_op jit(solution)/shard_map/ppermute | solution.py:54
  36.5 0.8 %collective-permute-start.9 = (f32[16,128]{1,0:T(8,128)S(1)}, f32[16,128]{1,0:T(8,128)S(1)}, u32[]{:S(2)}, u32[]{:S(2)}) collective-permute-start(f32[16,128]{1,0:T(8,128)S(1)} %get-tuple-element.33), channel_id=1, source_target_pairs={{0,12},{4,8},{8,4},{12,0},{1,13},{5,9},{9,5},{13,1},{2,14},{6,10},... | collective-permute-start | bytes 24584 | tf_op jit(solution)/shard_map/ppermute | solution.py:54
  38.1 3.8 %collective-permute-done.9.rest_3_ = f32[16,128]{1,0:T(8,128)S(1)} collective-permute-done((f32[16,128]{1,0:T(8,128)S(1)}, f32[16,128]{1,0:T(8,128)S(1)}, u32[]{:S(2)}, u32[]{:S(2)}) %collective-permute-start.9) | collective-permute-done | bytes 8224 | tf_op jit(solution)/shard_map/ppermute | solution.py:54
  41.9 1.4 %shard_map.147 = f32[256,128]{1,0:T(8,128)} custom-call(s32[1,4,16]{2,1,0:T(4,128)S(1)} %copy-done.8, s32[1,4]{1,0:T(1,128)S(1)} %copy-done.10, f32[16,128]{1,0:T(8,128)S(1)} %get-tuple-element.30.rest_0_, f32[16,128]{1,0:T(8,128)S(1)} %collective-permute-done.7.rest_1_, f32[16,128]{1,0:T(8,128)S(1)} %collective-permute-done.8.rest_2_, ...), custom_call_target="tpu_custom_call" | custom-call | tf_op jit(solution)/shard_map/pallas_call | solution.py:24
  (57 shorter events, 3.6 us)
Async XLA Ops:
  0.6 21.6 %copy-start.3 = (bf16[32,4,64]{2,1,0:T(4,128)(2,1)S(1)}, bf16[32,4,64]{2,1,0:T(4,128)(2,1)}, u32[]{:S(2)}) copy-start(bf16[32,4,64]{2,1,0:T(4,128)(2,1)} %param.16) | copy-start | bytes 49156
  0.6 0.8 %copy-start.4 = (bf16[256,128]{1,0:T(8,128)(2,1)S(1)}, bf16[256,128]{1,0:T(8,128)(2,1)}, u32[]{:S(2)}) copy-start(bf16[256,128]{1,0:T(8,128)(2,1)} %vol_ref.1) | copy-start | bytes 196612
  1.5 0.7 %copy-start.7 = (s32[1,4,16]{2,1,0:T(4,128)S(1)}, s32[1,4,16]{2,1,0:T(4,128)}, u32[]{:S(2)}) copy-start(s32[1,4,16]{2,1,0:T(4,128)} %req_ref.3) | copy-start | bytes 772
  2.2 0.7 %copy-start.9 = (s32[1,4]{1,0:T(1,128)S(1)}, s32[1,4]{1,0:T(1,128)}, u32[]{:S(2)}) copy-start(s32[1,4]{1,0:T(1,128)} %cnt_ref.3) | copy-start | bytes 52
  3.5 11.8 %collective-permute-start = (bf16[16,128]{1,0:T(8,128)(2,1)S(1)}, bf16[16,128]{1,0:T(8,128)(2,1)S(1)}, u32[]{:S(2)}, u32[]{:S(2)}) collective-permute-start(bf16[16,128]{1,0:T(8,128)(2,1)S(1)} %get-tuple-element.19), channel_id=1, source_target_pairs={{0,4},{4,0},{8,12},{12,8},{1,5},{5,1},{9,13},{13,9},{2,6},{6,2},{1... | collective-permute-start | bytes 12296 | tf_op jit(solution)/shard_map/ppermute | solution.py:54
  6.6 8.8 %collective-permute-start.1 = (bf16[16,128]{1,0:T(8,128)(2,1)S(1)}, bf16[16,128]{1,0:T(8,128)(2,1)S(1)}, u32[]{:S(2)}, u32[]{:S(2)}) collective-permute-start(bf16[16,128]{1,0:T(8,128)(2,1)S(1)} %get-tuple-element.20), channel_id=1, source_target_pairs={{0,8},{4,12},{8,0},{12,4},{1,9},{5,13},{9,1},{13,5},{2,10},{6,14},... | collective-permute-start | bytes 12296 | tf_op jit(solution)/shard_map/ppermute | solution.py:54
  9.2 6.2 %collective-permute-start.2 = (bf16[16,128]{1,0:T(8,128)(2,1)S(1)}, bf16[16,128]{1,0:T(8,128)(2,1)S(1)}, u32[]{:S(2)}, u32[]{:S(2)}) collective-permute-start(bf16[16,128]{1,0:T(8,128)(2,1)S(1)} %get-tuple-element.21), channel_id=1, source_target_pairs={{0,12},{4,8},{8,4},{12,0},{1,13},{5,9},{9,5},{13,1},{2,14},{6,10},... | collective-permute-start | bytes 12296 | tf_op jit(solution)/shard_map/ppermute | solution.py:54
  13.6 0.8 %copy-start.5 = (bf16[32,4,256]{2,1,0:T(4,128)(2,1)S(1)}, bf16[32,4,256]{2,1,0:T(4,128)(2,1)}, u32[]{:S(2)}) copy-start(bf16[32,4,256]{2,1,0:T(4,128)(2,1)} %dual_ref.1) | copy-start | bytes 196612
  14.4 0.8 %copy-start.6 = (bf16[32,4,256]{2,1,0:T(4,128)(2,1)S(1)}, bf16[32,4,256]{2,1,0:T(4,128)(2,1)}, u32[]{:S(2)}) copy-start(bf16[32,4,256]{2,1,0:T(4,128)(2,1)} %meas_ref.1) | copy-start | bytes 196612
  15.4 1.6 %copy-start = (bf16[32,128,256]{2,1,0:T(8,128)(2,1)S(1)}, bf16[32,128,256]{2,1,0:T(8,128)(2,1)}, u32[]{:S(2)}) copy-start(bf16[32,128,256]{2,1,0:T(8,128)(2,1)} %foot_ref.3) | copy-start | bytes 6291460
  17.0 0.8 %copy-start.2 = (bf16[32,4,64]{2,1,0:T(4,128)(2,1)S(1)}, bf16[32,4,64]{2,1,0:T(4,128)(2,1)}, u32[]{:S(2)}) copy-start(bf16[32,4,64]{2,1,0:T(4,128)(2,1)} %param.16) | copy-start | bytes 49156
  17.7 9.1 %copy-start.11 = (f32[32]{0:T(128)S(1)}, f32[32]{0:T(128)}, u32[]{:S(2)}) copy-start(f32[32]{0:T(128)} %param.21) | copy-start | bytes 388
  17.7 9.1 %copy-start.12 = (f32[32]{0:T(128)S(1)}, f32[32]{0:T(128)}, u32[]{:S(2)}) copy-start(f32[32]{0:T(128)} %param.23) | copy-start | bytes 388
  18.3 4.7 %collective-permute-start.3 = (bf16[16,1024]{1,0:T(8,128)(2,1)S(1)}, bf16[16,1024]{1,0:T(8,128)(2,1)S(1)}, u32[]{:S(2)}, u32[]{:S(2)}) collective-permute-start(bf16[16,1024]{1,0:T(8,128)(2,1)S(1)} %get-tuple-element.25), channel_id=1, source_target_pairs={{0,4},{4,0},{8,12},{12,8},{1,5},{5,1},{9,13},{13,9},{2,6},{6,2},{1... | collective-permute-start | bytes 98312 | tf_op jit(solution)/shard_map/ppermute | solution.py:47
  19.2 5.7 %collective-permute-start.4 = (bf16[16,1024]{1,0:T(8,128)(2,1)S(1)}, bf16[16,1024]{1,0:T(8,128)(2,1)S(1)}, u32[]{:S(2)}, u32[]{:S(2)}) collective-permute-start(bf16[16,1024]{1,0:T(8,128)(2,1)S(1)} %get-tuple-element.26), channel_id=1, source_target_pairs={{0,12},{4,8},{8,4},{12,0},{1,13},{5,9},{9,5},{13,1},{2,14},{6,10},... | collective-permute-start | bytes 98312 | tf_op jit(solution)/shard_map/ppermute | solution.py:47
  25.1 5.9 %collective-permute-start.5 = (bf16[3,48,128]{2,1,0:T(8,128)(2,1)S(1)}, bf16[3,48,128]{2,1,0:T(8,128)(2,1)S(1)}, u32[]{:S(2)}, u32[]{:S(2)}) collective-permute-start(bf16[3,48,128]{2,1,0:T(8,128)(2,1)S(1)} %get-tuple-element.28), channel_id=1, source_target_pairs={{0,1},{1,0},{2,3},{3,2},{4,5},{5,4},{6,7},{7,6},{8,9},{9,8},{10,11... | collective-permute-start | bytes 110600 | tf_op jit(solution)/shard_map/ppermute | solution.py:47
  25.2 5.8 %collective-permute-start.6 = (bf16[3,48,128]{2,1,0:T(8,128)(2,1)S(1)}, bf16[3,48,128]{2,1,0:T(8,128)(2,1)S(1)}, u32[]{:S(2)}, u32[]{:S(2)}) collective-permute-start(bf16[3,48,128]{2,1,0:T(8,128)(2,1)S(1)} %get-tuple-element.28), channel_id=1, source_target_pairs={{0,3},{1,2},{2,1},{3,0},{4,7},{5,6},{6,5},{7,4},{8,11},{9,10},{10,... | collective-permute-start | bytes 110600 | tf_op jit(solution)/shard_map/ppermute | solution.py:47
  26.9 4.0 %copy-start.1 = (bf16[32,128,256]{2,1,0:T(8,128)(2,1)S(1)}, bf16[32,128,256]{2,1,0:T(8,128)(2,1)}, u32[]{:S(2)}) copy-start(bf16[32,128,256]{2,1,0:T(8,128)(2,1)} %foot_ref.3) | copy-start | bytes 6291460
  30.9 11.0 %copy-start.8 = (s32[1,4,16]{2,1,0:T(4,128)S(1)}, s32[1,4,16]{2,1,0:T(4,128)}, u32[]{:S(2)}) copy-start(s32[1,4,16]{2,1,0:T(4,128)} %req_ref.3) | copy-start | bytes 772
  31.0 11.0 %copy-start.10 = (s32[1,4]{1,0:T(1,128)S(1)}, s32[1,4]{1,0:T(1,128)}, u32[]{:S(2)}) copy-start(s32[1,4]{1,0:T(1,128)} %cnt_ref.3) | copy-start | bytes 52
  32.9 5.1 %collective-permute-start.7 = (f32[16,128]{1,0:T(8,128)S(1)}, f32[16,128]{1,0:T(8,128)S(1)}, u32[]{:S(2)}, u32[]{:S(2)}) collective-permute-start(f32[16,128]{1,0:T(8,128)S(1)} %get-tuple-element.31), channel_id=1, source_target_pairs={{0,4},{4,0},{8,12},{12,8},{1,5},{5,1},{9,13},{13,9},{2,6},{6,2},{1... | collective-permute-start | bytes 24584 | tf_op jit(solution)/shard_map/ppermute | solution.py:54
  33.1 5.0 %collective-permute-start.8 = (f32[16,128]{1,0:T(8,128)S(1)}, f32[16,128]{1,0:T(8,128)S(1)}, u32[]{:S(2)}, u32[]{:S(2)}) collective-permute-start(f32[16,128]{1,0:T(8,128)S(1)} %get-tuple-element.32), channel_id=1, source_target_pairs={{0,8},{4,12},{8,0},{12,4},{1,9},{5,13},{9,1},{13,5},{2,10},{6,14},... | collective-permute-start | bytes 24584 | tf_op jit(solution)/shard_map/ppermute | solution.py:54
  36.5 5.4 %collective-permute-start.9 = (f32[16,128]{1,0:T(8,128)S(1)}, f32[16,128]{1,0:T(8,128)S(1)}, u32[]{:S(2)}, u32[]{:S(2)}) collective-permute-start(f32[16,128]{1,0:T(8,128)S(1)} %get-tuple-element.33), channel_id=1, source_target_pairs={{0,12},{4,8},{8,4},{12,0},{1,13},{5,9},{9,5},{13,1},{2,14},{6,10},... | collective-permute-start | bytes 24584 | tf_op jit(solution)/shard_map/ppermute | solution.py:54
where the time goes:
time: 43.8 us; the launch traced here: 43.3 us
  starting transfers between devices  15.7 us (36%)
  local copies, waits for them, and re-layouts  10.7 us (24%)
  Pallas kernels  8.89 us (20%)
  waiting for transfers between devices  6 us (14%)
  matrix products  1.12 us (3%)
  between operations  0.86 us (2%)
    ppermute x6, starting transfers between devices, exchange(): lax.ppermute(pieces[k], axis, [(i, i ^ k) for i in range(n)])  10.1 us
    pallas_call x8, Pallas kernels, call(): pl.pallas_call(body, out_shape=outs if single else list(outs), in_specs=s...  8.89 us
    unnamed x38, local copies, waits for them, and re-layouts  6.82 us
    ppermute x2, starting transfers between devices, both_ways(): lax.ppermute(array_b, axis, second)  4.61 us
    ppermute x6, waiting for transfers between devices, exchange(): lax.ppermute(pieces[k], axis, [(i, i ^ k) for i in range(n)])  3.97 us
    ppermute x2, waiting for transfers between devices, both_ways(): lax.ppermute(array_b, axis, second)  2.02 us
    dot_general x1, matrix products, banded_weights(): jnp.einsum('ok,vkn->von', first, move, preferred_element_type=F32)  1.12 us
    ppermute x2, starting transfers between devices, both_ways(): lax.ppermute(array_a, axis, first)  1.03 us
  transfers between devices with their start and end apart: 10, of which 3 were waited for; matrix products, arithmetic and copies ran while one was open for 13% of the time, Pallas kernels for 10%

commit v1 on v0

--- a/solution.py
+++ b/solution.py
@@ -2,7 +2,6 @@
 
 import jax
 import jax.numpy as jnp
-import numpy as np
 from jax import lax
 from jax.experimental import pallas as pl
 from jax.experimental.pallas import tpu as pltpu
@@ -12,9 +11,8 @@
 BAND = 8
 STEP = 6
 LANES = 128
-EDGE_ROWS = 16
 VM = pl.BlockSpec(memory_space=pltpu.VMEM)
-SM = pl.BlockSpec(memory_space=pltpu.SMEM)
+HBM = pl.BlockSpec(memory_space=pltpu.HBM)
 F32 = jnp.float32
 BF16 = jnp.bfloat16
 
@@ -32,6 +30,10 @@
     )(*args)
 
 
+def from_hbm(arrays):
+    return [pltpu.with_memory_space_constraint(x, pltpu.HBM) for x in arrays]
+
+
 def shape(dims, dtype=F32):
     return jax.ShapeDtypeStruct(dims, dtype)
 
@@ -54,47 +56,61 @@
     return [pieces[0]] + [lax.ppermute(pieces[k], axis, [(i, i ^ k) for i in range(n)]) for k in range(1, n)]
 
 
-def gather_kernel(n, slots, split, req_ref, cnt_ref, vol_ref, *rest):
-    outs, (vol_s, out_s) = rest[:-2], rest[-2:]
-    tiles = vol_ref.shape[0]
-    vol_s[0:tiles, :] = vol_ref[...].astype(F32)
-    vol_s[tiles : tiles + 8, :] = jnp.zeros((8, vol_ref.shape[1]), F32)
+def iota(shape_, dim):
+    return lax.broadcasted_iota(jnp.int32, shape_, dim)
+
+
+def as_column(row):
+    m = row.shape[1]
+    spread = jnp.broadcast_to(row, (m, m))
+    return jnp.sum(jnp.where(iota((m, m), 0) == iota((m, m), 1), spread, 0.0), axis=1, keepdims=True)
+
+
+def wanted_row(req_ref, cnt_ref, dest):
+    slots, n = req_ref.shape[2], cnt_ref.shape[1]
+    row = req_ref[0, pl.ds(dest, 1), :].astype(F32)
+    count = jnp.sum(jnp.where(iota((1, n), 1) == dest, cnt_ref[...].astype(F32), 0.0), axis=1, keepdims=True)
+    return jnp.where(iota((1, slots), 1).astype(F32) < count, row, -1.0)
+
+
+def fetch(pairs, sems):
+    copies = [pltpu.make_async_copy(src, dst, sems.at[i]) for i, (src, dst) in enumerate(pairs)]
+    for copy in copies:
+        copy.start()
+    return copies
+
+
+def gather_kernel(n, slots, split, req_hbm, cnt_hbm, vol_hbm, *rest):
+    outs, (req, cnt, vol, sems) = rest[:-4], rest[-4:]
+    copies = fetch([(req_hbm, req), (cnt_hbm, cnt), (vol_hbm, vol)], sems)
+    tiles = vol.shape[0]
     me = lax.axis_index("view")
-
-    def chunk(k, dest):
-        count = cnt_ref[0, dest]
-        for s in range(slots):
-            row = jnp.where(s < count, req_ref[0, dest, s], tiles)
-            out_s[pl.ds(k * slots + s, 1), :] = vol_s[pl.ds(row, 1), :]
-
-    if split:
-        for k in range(n):
-            chunk(k, me ^ k)
-            outs[k][...] = out_s[k * slots : (k + 1) * slots, :].astype(BF16)
-    else:
-        lax.fori_loop(0, n, lambda k, c: (chunk(k, k), c)[1], 0)
-        outs[0][...] = out_s[...].astype(BF16)
-
-
-def scatter_kernel(n, slots, split, req_ref, cnt_ref, *rest):
-    pieces, out_ref, acc = rest[:-2], rest[-2], rest[-1]
-    tiles = out_ref.shape[0]
-    acc[...] = jnp.zeros(acc.shape, F32)
-    me = lax.axis_index("view")
-
-    def chunk(source, dest):
-        count = cnt_ref[0, dest]
-        rows = [jnp.where(s < count, req_ref[0, dest, s], tiles) for s in range(slots)]
-        sums = [acc[pl.ds(rows[s], 1), :] + source(s) for s in range(slots)]
-        for s in range(slots):
-            acc[pl.ds(rows[s], 1), :] = sums[s]
-
-    if split:
-        for k in range(n):
-            chunk(lambda s: pieces[k][s : s + 1, :], me ^ k)
-    else:
-        lax.fori_loop(0, n, lambda k, c: (chunk(lambda s: pieces[0][pl.ds(k * slots + s, 1), :], k), c)[1], 0)
-    out_ref[...] = acc[0:tiles, :]
+    copies[0].wait()
+    copies[1].wait()
+    picks = []
+    for k in range(n):
+        column = as_column(wanted_row(req, cnt, me ^ k if split else k))
+        hit = iota((slots, tiles), 1).astype(F32) == column
+        picks.append(jnp.where(hit, 1.0, 0.0).astype(BF16))
+    copies[2].wait()
+    for k in range(n):
+        got = jnp.dot(picks[k], vol[...], preferred_element_type=F32).astype(BF16)
+        if split:
+            outs[k][...] = got
+        else:
+            outs[0][k * slots : (k + 1) * slots, :] = got
+
+
+def scatter_kernel(hot_ref, *rest):
+    pieces, out_ref = rest[:-1], rest[-1]
+    left = jnp.concatenate([p[...] for p in pieces], axis=0)
+    total = None
+    for _ in range(3):
+        part = left.astype(BF16)
+        left = left - part.astype(F32)
+        got = jnp.dot(hot_ref[...], part, preferred_element_type=F32)
+        total = got if total is None else total + got
+    out_ref[...] = total
 
 
 def put_flat(flat_ref, start, block):
@@ -109,12 +125,65 @@
     )
 
 
-def widen_kernel(dual_ref, meas_ref, out_ref, flat):
-    views, rows, _ = dual_ref.shape
-    for i, ref in enumerate((dual_ref, meas_ref)):
+def network_weights(first, second, last, w1_ref, w2_ref, w3_ref):
+    channels = second.shape[3]
+    sub, view = iota((16, BAND * channels), 0), iota((16, BAND * channels), 1) // channels
+    blocks = []
+    for b in range(3):
+        for c in range(3):
+            block = jnp.zeros(sub.shape, F32)
+            for a in range(3):
+                row = first[a, b].astype(F32)[c : c + 1, :]
+                block = jnp.where(sub == view + a, jnp.concatenate([row] * BAND, axis=1), block)
+            blocks.append(block)
+    depth = 16 * len(blocks)
+    blocks.append(jnp.zeros((-depth % LANES, BAND * channels), F32))
+    w1_ref[...] = jnp.concatenate(blocks, axis=0).T[:, 0:depth].astype(BF16)
+    full = (STEP + 2) * channels
+    for b in range(3):
+        taps = [second[a, b].astype(F32) for a in range(3)]
+        wide = jnp.concatenate(taps + [jnp.zeros((channels, full - 3 * channels), F32)], axis=1)
+        for v in range(STEP):
+            at = slice(v * channels, (v + 1) * channels)
+            w2_ref[at, b * full : (b + 1) * full] = pltpu.roll(wide, v * channels, 1).astype(BF16)
+    out = []
+    sub = iota((8, full), 0)
+    for b in range(3):
+        taps = [last[a].astype(F32)[b : b + 1, :] for a in range(3)]
+        wide = jnp.concatenate(taps + [jnp.zeros((1, full - 3 * channels), F32)], axis=1)
+        wide = jnp.broadcast_to(wide, (8, full))
+        block = jnp.zeros((8, full), F32)
+        for v in range(STEP):
+            block = jnp.where(sub == v, pltpu.roll(wide, v * channels, 1), block)
+        out.append(block)
+    w3_ref[...] = jnp.concatenate(out, axis=0).astype(BF16)
+
+
+def setup_kernel(n, split, *refs):
+    ins, outs, (sems, flat, ax_flat), local = refs[:11], refs[11:21], refs[21:24], refs[24:]
+    stat_ref, foot_ref, ax_ref, back_ref, w1_ref, w2_ref, w3_ref, a1_ref, a2_ref, hot_ref = outs
+    dual, meas, axial, first, second, last, slopes_1, slopes_2, req, cnt = local
+    copies = fetch(list(zip(ins, (*local, foot_ref))), sems)
+    for copy in copies[:-1]:
+        copy.wait()
+    views, rows, slots = axial.shape
+    for i, ref in enumerate((dual, meas)):
         for v in range(views):
             put_flat(flat, v * rows, ref[v].astype(F32))
-        out_ref[i] = widen(flat, rows)
+        stat_ref[i] = widen(flat, rows)
+    ax_flat[...] = jnp.zeros(ax_flat.shape, F32)
+    for v in range(views):
+        ax_flat[v * rows : (v + 1) * rows, 0:slots] = axial[v].astype(F32)
+    ax_ref[...] = ax_flat[:, 0:slots].astype(BF16)
+    back_ref[...] = ax_flat[...].T[0:slots, :].astype(BF16)
+    network_weights(first, second, last, w1_ref, w2_ref, w3_ref)
+    for ref, out in ((slopes_1, a1_ref), (slopes_2, a2_ref)):
+        out[...] = jnp.broadcast_to(as_column(ref[...]), out.shape)
+    me = lax.axis_index("view")
+    row = jnp.concatenate([wanted_row(req, cnt, me ^ k if split else k) for k in range(n)], axis=1)
+    hit = iota(hot_ref.shape, 0).astype(F32) == row
+    hot_ref[...] = jnp.where(hit, 1.0, 0.0).astype(BF16)
+    copies[-1].wait()
 
 
 def forward_kernel(n, rows, axial_ref, foot_ref, stat_ref, *rest):
@@ -144,28 +213,30 @@
     for way, start in ((0, 0), (1, views - HALO)):
         for c in range(3):
             part = fw[start : start + HALO, :] if c == 1 else stat_ref[c // 2, start : start + HALO, :]
-            edge[way, c * HALO : (c + 1) * HALO, :] = part
+            for t in range(part.shape[1] // LANES):
+                at = (3 * t + c) * HALO
+                edge[way, at : at + HALO, :] = part[:, t * LANES : (t + 1) * LANES]
     even = me % 2 == 0
     to_prev, to_next = edge[0], edge[1]
     a_ref[...] = jnp.where(even, to_next, to_prev).astype(BF16)
     b_ref[...] = jnp.where(even, to_prev, to_next).astype(BF16)
 
 
-def halo_of(a_ref, b_ref, channel):
+def sort_halo(a_ref, b_ref, halo):
     even = lax.axis_index("view") % 2 == 0
-    rows = slice(channel * HALO, (channel + 1) * HALO)
-    a = a_ref[...].astype(F32)[rows]
-    b = b_ref[...].astype(F32)[rows]
-    return jnp.where(even, b, a), jnp.where(even, a, b)
-
-
-def lane(shape_):
-    return lax.broadcasted_iota(jnp.int32, shape_, 1)
+    a, b = a_ref[...].astype(F32), b_ref[...].astype(F32)
+    halo[0] = jnp.where(even, b, a)
+    halo[1] = jnp.where(even, a, b)
+
+
+def halo_of(halo, way, channel, wide):
+    starts = [(3 * t + channel) * HALO for t in range(wide // LANES)]
+    return jnp.concatenate([halo[way, at : at + HALO, :] for at in starts], axis=1)
 
 
 def strip_of(wide, rows, inner):
     cols = wide.shape[1] // rows
-    at = lane((wide.shape[0], LANES))
+    at = iota((wide.shape[0], LANES), 1)
     total = jnp.zeros((wide.shape[0], LANES), F32)
     for r in range(rows):
         head = wide[:, r * cols : r * cols + LANES]
@@ -188,17 +259,20 @@
         msg_ref[c] = strip_of(wide, rows, False)
 
 
-def strip_message_kernel(rows, in_ref, msg_ref, a_ref, b_ref, strip_ref, out_ref, buf):
+def strip_message_kernel(rows, wide, in_ref, msg_ref, a_ref, b_ref, strip_ref, out_ref, buf, halo):
     views = in_ref.shape[1]
+    sort_halo(a_ref, b_ref, halo)
     buf[...] = jnp.zeros(buf.shape, F32)
     strip_ref[...] = jnp.zeros(strip_ref.shape, F32)
     for c in range(3):
-        for start, part in zip((0, HALO + views), halo_of(a_ref, b_ref, c)):
+        for way, start in ((0, 0), (1, HALO + views)):
+            part = halo_of(halo, way, c, wide)
             strip_ref[c, start : start + HALO, :] = strip_of(part, rows, True)
             buf[c, start : start + HALO, :] = strip_of(part, rows, False)
         strip_ref[c, HALO : HALO + views, :] = in_ref[c]
         buf[c, HALO : HALO + views, :] = msg_ref[c]
-        out_ref[c] = buf[c].astype(BF16)
+    total = buf[0] + pltpu.roll(buf[1], HALO, 1) + pltpu.roll(buf[2], 2 * HALO, 1)
+    out_ref[...] = total.astype(BF16)
 
 
 def prelu(z, slopes_ref):
@@ -254,11 +328,12 @@
         update[STEP * k : STEP * k + count, :] = out[0:count, :]
 
 
-def main_kernel(rows, fw_ref, stat_ref, ha_ref, hb_ref, w1, w2, w3, a1, a2, out_ref, x, s1, s2, s3, update):
-    views = fw_ref.shape[0]
+def main_kernel(rows, fw_ref, stat_ref, ha_ref, hb_ref, w1, w2, w3, a1, a2, out_ref, x, halo, s1, s2, s3, update):
+    views, wide = fw_ref.shape
+    sort_halo(ha_ref, hb_ref, halo)
     x[...] = jnp.zeros(x.shape, F32)
     for c in range(3):
-        before, after = halo_of(ha_ref, hb_ref, c)
+        before, after = halo_of(halo, 0, c, wide), halo_of(halo, 1, c, wide)
         x[c, 0:HALO, :] = before
         x[c, HALO : HALO + views, :] = fw_ref[...] if c == 1 else stat_ref[c // 2]
         x[c, HALO + views : 2 * HALO + views, :] = after
@@ -276,19 +351,19 @@
     views, _, cols = foot_ref.shape[0], foot_ref.shape[1], foot_ref.shape[2]
     me, peers = lax.axis_index("col"), lax.axis_size("col")
     even = me % 2 == 0
-    at = lane((1, LANES))
+    at = iota((1, LANES), 1)
     left_side, step = at < 64, at % 16
     from_left = left_side & (step < HALO) & (me > 0)
     from_right = (~left_side) & (step >= 6) & (step < 9) & (me < peers - 1)
     inside = (left_side & ((step >= HALO) | (me > 0))) | ((~left_side) & ((step < 6) | (me < peers - 1)))
+    a, b = ra_ref[...].astype(F32), rb_ref[...].astype(F32)
+    sides = jnp.where(at < 64, jnp.where(even, b, a), jnp.where(even, a, b))
     for c in range(3):
-        a, b = ra_ref[c].astype(F32), rb_ref[c].astype(F32)
-        right = jnp.where(even, a, b)
-        left = jnp.where(even, b, a)
-        x[c] = jnp.where(from_left, left, jnp.where(from_right, right, strip_ref[c]))
+        side = pltpu.roll(sides, (-HALO * c) % LANES, 1)
+        x[c] = jnp.where(from_left | from_right, side, strip_ref[c])
     network(lambda c: x[c], views, w1, w2, w3, a1, a2, s1, s2, s3, update, inside)
     strip = x[0, HALO : HALO + views, :] + update[...]
-    first = lane((views, LANES))
+    first = iota((views, LANES), 1)
     for r in range(rows):
         head = main_ref[:, r * cols : r * cols + LANES]
         tail = main_ref[:, (r + 1) * cols - LANES : (r + 1) * cols]
@@ -323,35 +398,6 @@
         parts[0][...] = partial
 
 
-def banded_weights(conv_first, conv_second, conv_last):
-    channels = conv_second.shape[3]
-    move = np.zeros((BAND, 3, 3, 3, 3, 3, 16), np.float32)
-    for v in range(BAND):
-        for a in range(3):
-            for b in range(3):
-                for c in range(3):
-                    move[v, b, c, a, b, c, v + a] = 1.0
-    move = jnp.asarray(move.reshape(BAND, 27, 144), BF16)
-    first = conv_first.transpose(2, 1, 3, 0).reshape(channels, 27)
-    w1 = jnp.einsum("ok,vkn->von", first, move, preferred_element_type=F32).astype(BF16)
-    w1 = w1.reshape(BAND * channels, 144)
-
-    def slide(w, steps):
-        return jnp.stack(
-            [
-                jnp.pad(w, [(0, 0)] * (w.ndim - 1) + [(v * channels, (STEP - 1 - v) * channels)])
-                for v in range(steps)
-            ]
-        )
-
-    second = conv_second.transpose(1, 2, 0, 3).reshape(3, channels, 3 * channels)
-    w2 = slide(second, STEP).transpose(0, 2, 1, 3).reshape(STEP * channels, 3 * (STEP + 2) * channels)
-    last = conv_last.transpose(1, 2, 0, 3).reshape(3, 3 * channels)
-    w3 = slide(last, STEP).transpose(1, 0, 2)
-    w3 = jnp.pad(w3, ((0, 0), (0, 8 - STEP), (0, 0))).reshape(24, (STEP + 2) * channels)
-    return w1, w2, w3
-
-
 def shards(
     volume,
     requests,
@@ -373,42 +419,80 @@
     wide = rows * cols
     channels = conv_second.shape[2]
     split = n in (2, 4)
+    dma = pltpu.SemaphoreType.DMA
     pieces = [shape((slots, vox), BF16)] * n if split else [shape((n * slots, vox), BF16)]
     outgoing = call(
         functools.partial(gather_kernel, n, slots, split),
         pieces,
-        [pltpu.VMEM((tiles + 8, vox), F32), pltpu.VMEM((n * slots, vox), F32)],
-        [requests, counts, volume],
-        [SM, SM, VM],
+        [
+            pltpu.VMEM(requests.shape, jnp.int32),
+            pltpu.VMEM(counts.shape, jnp.int32),
+            pltpu.VMEM(volume.shape, BF16),
+            dma((3,)),
+        ],
+        from_hbm([requests, counts, volume]),
+        [HBM] * 3,
     )
     incoming = exchange(outgoing, "view")
 
-    stat = call(widen_kernel, shape((2, views, wide)), [pltpu.VMEM((cols // LANES, views * rows, LANES), F32)], [dual, measured])
-    w1, w2, w3 = banded_weights(conv_first, conv_second, conv_last)
-    a1 = jnp.broadcast_to(slopes_first[:, None], (channels, LANES))
-    a2 = jnp.broadcast_to(slopes_second[:, None], (channels, LANES))
-    axial_flat = axial.reshape(views * rows, n * slots)
-    axial_back = axial_flat.T
-
-    edge = shape((EDGE_ROWS, wide), BF16)
+    small = [
+        dual,
+        measured,
+        axial,
+        conv_first.transpose(0, 1, 3, 2),
+        conv_second,
+        conv_last.reshape(3, 3, channels),
+        slopes_first.reshape(1, channels),
+        slopes_second.reshape(1, channels),
+        requests,
+        counts,
+    ]
+    flat = pltpu.VMEM((cols // LANES, views * rows, LANES), F32)
+    full = (STEP + 2) * channels
+    stat, foot, axial_flat, axial_back, w1, w2, w3, a1, a2, hot = call(
+        functools.partial(setup_kernel, n, split),
+        [
+            shape((2, views, wide)),
+            shape(footprint.shape, BF16),
+            shape((views * rows, n * slots), BF16),
+            shape((n * slots, views * rows), BF16),
+            shape((BAND * channels, 144), BF16),
+            shape((STEP * channels, 3 * full), BF16),
+            shape((24, full), BF16),
+            shape((channels, LANES)),
+            shape((channels, LANES)),
+            shape((tiles, n * slots), BF16),
+        ],
+        [
+            dma((len(small) + 1,)),
+            flat,
+            pltpu.VMEM((views * rows, -(-n * slots // LANES) * LANES), F32),
+            *[pltpu.VMEM(x.shape, x.dtype) for x in small],
+        ],
+        from_hbm([*small, footprint]),
+        [HBM] * (len(small) + 1),
+        cost=(10**8, 4 * 10**6),
+    )
+
+    message_rows = -(-9 * (wide // LANES) // 16) * 16
+    edge = shape((message_rows, LANES), BF16)
+    halo = pltpu.VMEM((2, message_rows, LANES), F32)
     fw, edge_a, edge_b = call(
         functools.partial(forward_kernel, n, rows),
         [shape((views, wide)), edge, edge],
-        [
-            pltpu.VMEM((n * slots, vox), BF16),
-            pltpu.VMEM((cols // LANES, views * rows, LANES), F32),
-            pltpu.VMEM((2, EDGE_ROWS, wide), F32),
-        ],
-        [axial_flat, footprint, stat, *incoming],
+        [pltpu.VMEM((n * slots, vox), BF16), flat, halo],
+        [axial_flat, foot, stat, *incoming],
     )
     halo_a, halo_b = both_ways(edge_a, edge_b, "view")
     own = shape((3, views, LANES))
-    strip_in, strip_msg = call(functools.partial(own_strip_kernel, rows), [own, own], [], [fw, stat])
+    strip_in, strip_msg = call(
+        functools.partial(own_strip_kernel, rows), [own, own], [], [fw, stat], cost=(10**7, 10**6)
+    )
     padded = 48
     strip, message = call(
-        functools.partial(strip_message_kernel, rows),
-        [shape((3, padded, LANES)), shape((3, padded, LANES), BF16)],
-        [pltpu.VMEM((3, padded, LANES), F32)],
+        functools.partial(strip_message_kernel, rows, wide),
+        [shape((3, padded, LANES)), shape((padded, LANES), BF16)],
+        [pltpu.VMEM((3, padded, LANES), F32), halo],
         [strip_in, strip_msg, halo_a, halo_b],
     )
     side_a, side_b = both_ways(message, message, "col")
@@ -424,7 +508,7 @@
     main = call(
         functools.partial(main_kernel, rows),
         shape((views, wide)),
-        [pltpu.VMEM((3, padded, wide), F32), *net_scratch(cols)],
+        [pltpu.VMEM((3, padded, wide), F32), halo, *net_scratch(cols)],
         [fw, stat, halo_a, halo_b, w1, w2, w3, a1, a2],
         cost=(2 * 10**9, 4 * 10**6),
     )
@@ -435,20 +519,14 @@
         [
             pltpu.VMEM((3, padded, LANES), F32),
             *net_scratch(LANES),
-            pltpu.VMEM((cols // LANES, views * rows, LANES), F32),
+            flat,
             pltpu.VMEM((views * rows, vox), BF16),
             pltpu.VMEM((n * slots, vox), F32),
         ],
-        [strip, side_a, side_b, w1, w2, w3, a1, a2, main, footprint, axial_back],
+        [strip, side_a, side_b, w1, w2, w3, a1, a2, main, foot, axial_back],
     )
     arrived = exchange(returned, "view")
-    backprojection = call(
-        functools.partial(scatter_kernel, n, slots, split),
-        shape((tiles, vox)),
-        [pltpu.VMEM((tiles + 8, vox), F32)],
-        [requests, counts, *arrived],
-        [SM, SM] + [VM] * len(arrived),
-    )
+    backprojection = call(scatter_kernel, shape((tiles, vox)), [], [hot, *arrived])
     return dual_out.reshape(views, rows, cols), backprojection
 
 

time: 43.8 us -> 34.7 us (0.79)
  local copies, waits for them, and re-layouts: 10.7 us -> 0.65 us
  waiting for transfers between devices: 6 us -> 9.82 us
  starting transfers between devices: 15.7 us -> 12.3 us
  Pallas kernels: 8.89 us -> 11 us
  matrix products: 1.12 us -> 0 us
    unnamed x38 -> x0, local copies, waits for them, and re-layouts: 6.82 us -> none
    ppermute x2, starting transfers between devices: 4.61 us -> 0.59 us  [both_ways(): lax.ppermute(array_b, axis, second)]
    ppermute x2, waiting for transfers between devices: 0.01 us -> 2.94 us  [both_ways(): lax.ppermute(array_a, axis, first)]
    transpose x4 -> x0, local copies, waits for them, and re-layouts: 2.59 us -> none  [the longest x1 0.94 us: banded_weights(): conv_second.transpose(1, 2, 0, 3).reshape(3, channels, 3 * channels)]
    pallas_call x8, Pallas kernels: 8.89 us -> 11 us  [call(): pl.pallas_call(body, out_shape=outs if single else list(outs), in_specs=s...]
    dot_general x1 -> x0, matrix products: 1.12 us -> none  [banded_weights(): jnp.einsum('ok,vkn->von', first, move, preferred_element_type=F32)]
    ppermute x6, waiting for transfers between devices: 3.97 us -> 5 us  [exchange(): lax.ppermute(pieces[k], axis, [(i, i ^ k) for i in range(n)])]
    ppermute x2, starting transfers between devices: 1.03 us -> 1.66 us  [both_ways(): lax.ppermute(array_a, axis, first)]
  transfers between devices with their start and end apart: 10 -> 10, of which waited for: 3 -> 4; matrix products, arithmetic and copies ran while one was open for 13% -> 2% of each run, Pallas kernels for 10% -> 18%
where the time goes in v1:
time: 34.7 us; the launch traced here: 34.5 us
  starting transfers between devices  12.3 us (35%)
  Pallas kernels  11 us (32%)
  waiting for transfers between devices  9.82 us (28%)
  between operations  0.72 us (2%)
  local copies, waits for them, and re-layouts  0.65 us (2%)
    pallas_call x8, Pallas kernels, call(): pl.pallas_call(body, out_shape=outs if single else list(outs), in_specs=s...  11 us
    ppermute x6, starting transfers between devices, exchange(): lax.ppermute(pieces[k], axis, [(i, i ^ k) for i in range(n)])  10.1 us
    ppermute x6, waiting for transfers between devices, exchange(): lax.ppermute(pieces[k], axis, [(i, i ^ k) for i in range(n)])  5 us
    ppermute x2, waiting for transfers between devices, both_ways(): lax.ppermute(array_a, axis, first)  2.94 us
    ppermute x2, waiting for transfers between devices, both_ways(): lax.ppermute(array_b, axis, second)  1.88 us
    ppermute x2, starting transfers between devices, both_ways(): lax.ppermute(array_a, axis, first)  1.66 us
  transfers between devices with their start and end apart: 10, of which 4 were waited for; matrix products, arithmetic and copies ran while one was open for 2% of the time, Pallas kernels for 18%

profile of v1, /device:TPU:0, one launch (start us, length us, event | category | flops | bytes accessed | tf_op | source)
XLA Modules:
  0.0 34.5 jit_solution(906788846806217580)
XLA Ops:
  0.6 1.1 %shard_map.132 = (bf16[16,128]{1,0:T(8,128)(2,1)S(1)}, bf16[16,128]{1,0:T(8,128)(2,1)S(1)}, bf16[16,128]{1,0:T(8,128)(2,1)S(1)}, bf16[16,128]{1,0:T(8,128)(2,1)S(1)}) custom-call(s32[1,4,16]{2,1,0:T(4,128)} %req_hbm.1, s32[1,4]{1,0:T(1,128)} %cnt_hbm.1, bf16[256,128]{1,0:T(8,128)(2,1)} %vol_hbm.1), custom_call_target="tpu_custom_call" | custom-call | tf_op jit(solution)/shard_map/pallas_call | solution.py:22
  1.7 3.1 %collective-permute-start = (bf16[16,128]{1,0:T(8,128)(2,1)S(1)}, bf16[16,128]{1,0:T(8,128)(2,1)S(1)}, u32[]{:S(2)}, u32[]{:S(2)}) collective-permute-start(bf16[16,128]{1,0:T(8,128)(2,1)S(1)} %get-tuple-element.32), channel_id=1, source_target_pairs={{0,4},{4,0},{8,12},{12,8},{1,5},{5,1},{9,13},{13,9},{2,6},{6,2},{1... | collective-permute-start | bytes 12296 | tf_op jit(solution)/shard_map/ppermute | solution.py:56
  4.8 2.6 %collective-permute-start.1 = (bf16[16,128]{1,0:T(8,128)(2,1)S(1)}, bf16[16,128]{1,0:T(8,128)(2,1)S(1)}, u32[]{:S(2)}, u32[]{:S(2)}) collective-permute-start(bf16[16,128]{1,0:T(8,128)(2,1)S(1)} %get-tuple-element.33), channel_id=1, source_target_pairs={{0,8},{4,12},{8,0},{12,4},{1,9},{5,13},{9,1},{13,5},{2,10},{6,14},... | collective-permute-start | bytes 12296 | tf_op jit(solution)/shard_map/ppermute | solution.py:56
  7.4 0.0 collective-permute-start.2
  7.4 2.0 %shard_map.131 = (f32[2,32,1024]{2,1,0:T(8,128)S(1)}, bf16[32,128,256]{2,1,0:T(8,128)(2,1)S(1)}, bf16[128,64]{1,0:T(8,128)(2,1)S(1)}, bf16[64,128]{1,0:T(8,128)(...) custom-call(bf16[32,4,256]{2,1,0:T(4,128)(2,1)} %refs_0_.1, ...), custom_call_target="tpu_custom_call" | custom-call | flops 100000000 | bytes 4000000 | tf_op jit(solution)/shard_map/pallas_call | solution.py:22
  9.3 0.0 collective-permute-done.rest_1_
  9.4 3.4 %collective-permute-done.2.rest_3_ = bf16[16,128]{1,0:T(8,128)(2,1)S(1)} collective-permute-done((bf16[16,128]{1,0:T(8,128)(2,1)S(1)}, bf16[16,128]{1,0:T(8,128)(2,1)S(1)}, u32[]{:S(2)}, u32[]{:S(2)}) %collective-permute-start.2) | collective-permute-done | bytes 4128 | tf_op jit(solution)/shard_map/ppermute | solution.py:56
  12.8 0.5 %shard_map.133 = (f32[32,1024]{1,0:T(8,128)S(1)}, bf16[80,128]{1,0:T(8,128)(2,1)S(1)}, bf16[80,128]{1,0:T(8,128)(2,1)S(1)}) custom-call(bf16[128,64]{1,0:T(8,128)(2,1)S(1)} %get-tuple-element.28.axial_ref, bf16[32,128,256]{2,1,0:T(8,128)(2,1)S(1)} %get-tuple-element.29.foot_ref, f32[2,32,1024]{2,1,0:T(8,128)S(1)} %get-tuple-element.30.stat_ref, ...), custom_call_target="tpu_custom_call" | custom-call | tf_op jit(solution)/shard_map/pallas_call | solution.py:22
  13.3 0.1 collective-permute-start.3
  13.4 0.6 %collective-permute-start.4 = (bf16[80,128]{1,0:T(8,128)(2,1)S(1)}, bf16[80,128]{1,0:T(8,128)(2,1)S(1)}, u32[]{:S(2)}, u32[]{:S(2)}) collective-permute-start(bf16[80,128]{1,0:T(8,128)(2,1)S(1)} %get-tuple-element.39), channel_id=1, source_target_pairs={{0,12},{4,8},{8,4},{12,0},{1,13},{5,9},{9,5},{13,1},{2,14},{6,10},... | collective-permute-start | bytes 61448 | tf_op jit(solution)/shard_map/ppermute | solution.py:49
  13.9 0.3 shard_map.134
  14.2 2.9 %collective-permute-done.3.a_ref.ha_ref = bf16[80,128]{1,0:T(8,128)(2,1)S(1)} collective-permute-done((bf16[80,128]{1,0:T(8,128)(2,1)S(1)}, bf16[80,128]{1,0:T(8,128)(2,1)S(1)}, u32[]{:S(2)}, u32[]{:S(2)}) %collective-permute-start.3) | collective-permute-done | bytes 20512 | tf_op jit(solution)/shard_map/ppermute | solution.py:49
  17.2 1.9 %collective-permute-done.4.b_ref.hb_ref = bf16[80,128]{1,0:T(8,128)(2,1)S(1)} collective-permute-done((bf16[80,128]{1,0:T(8,128)(2,1)S(1)}, bf16[80,128]{1,0:T(8,128)(2,1)S(1)}, u32[]{:S(2)}, u32[]{:S(2)}) %collective-permute-start.4) | collective-permute-done | bytes 20512 | tf_op jit(solution)/shard_map/ppermute | solution.py:49
  19.0 0.2 shard_map.135
  19.2 0.0 collective-permute-start.6
  19.3 1.6 %collective-permute-start.5 = (bf16[48,128]{1,0:T(8,128)(2,1)S(1)}, bf16[48,128]{1,0:T(8,128)(2,1)S(1)}, u32[]{:S(2)}, u32[]{:S(2)}) collective-permute-start(bf16[48,128]{1,0:T(8,128)(2,1)S(1)} %get-tuple-element.41), channel_id=1, source_target_pairs={{0,1},{1,0},{2,3},{3,2},{4,5},{5,4},{6,7},{7,6},{8,9},{9,8},{10,11... | collective-permute-start | bytes 36872 | tf_op jit(solution)/shard_map/ppermute | solution.py:49
  20.9 4.2 %shard_map.136.main_ref = f32[32,1024]{1,0:T(8,128)S(1)} custom-call(f32[32,1024]{1,0:T(8,128)S(1)} %get-tuple-element.35.fw_ref, f32[2,32,1024]{2,1,0:T(8,128)S(1)} %get-tuple-element.30.stat_ref, bf16[80,128]{1,0:T(8,128)(2,1)S(1)} %collective-permute-done.3.a_ref.ha_ref, bf16[80,128]{1,0:T(8,128)(2,1)S(1)} %collective-permute-done.4.b_ref.hb_ref, ...), custom_call_target="tpu_custom_call" | custom-call | flops 2000000000 | bytes 4000000 | tf_op jit(solution)/shard_map/pallas_call | solution.py:22
  25.1 2.0 %shard_map.137 = (bf16[128,256]{1,0:T(8,128)(2,1)S(1)}, f32[16,128]{1,0:T(8,128)S(1)}, f32[16,128]{1,0:T(8,128)S(1)}, f32[16,128]{1,0:T(8,128)S(1)}, f32[16,128]{1,0:T(8,128)S(1)}) custom-call(f32[3,48,128]{2,1,0:T(8,128)S(1)} %get-tuple-element.40.strip_ref, bf16[48,128]{1,0:T(8,128)(2,1)S(1)} %collective-permute-done.5.ra_ref, ...), custom_call_target="tpu_custom_call" | custom-call | tf_op jit(solution)/shard_map/pallas_call | solution.py:22
  27.1 0.2 collective-permute-start.7
  27.2 1.0 %collective-permute-start.8 = (f32[16,128]{1,0:T(8,128)S(1)}, f32[16,128]{1,0:T(8,128)S(1)}, u32[]{:S(2)}, u32[]{:S(2)}) collective-permute-start(f32[16,128]{1,0:T(8,128)S(1)} %get-tuple-element.52), channel_id=1, source_target_pairs={{0,8},{4,12},{8,0},{12,4},{1,9},{5,13},{9,1},{13,5},{2,10},{6,14},... | collective-permute-start | bytes 24584 | tf_op jit(solution)/shard_map/ppermute | solution.py:56
  28.2 3.2 %collective-permute-start.9 = (f32[16,128]{1,0:T(8,128)S(1)}, f32[16,128]{1,0:T(8,128)S(1)}, u32[]{:S(2)}, u32[]{:S(2)}) collective-permute-start(f32[16,128]{1,0:T(8,128)S(1)} %get-tuple-element.53), channel_id=1, source_target_pairs={{0,12},{4,8},{8,4},{12,0},{1,13},{5,9},{9,5},{13,1},{2,14},{6,10},... | collective-permute-start | bytes 24584 | tf_op jit(solution)/shard_map/ppermute | solution.py:56
  31.5 0.6 %reshape.19 = bf16[32,4,256]{2,1,0:T(4,128)(2,1)} reshape(bf16[128,256]{1,0:T(8,128)(2,1)S(1)} %get-tuple-element.48) | data formatting | bytes 131072 | tf_op jit(solution)/shard_map/reshape | solution.py:530
  32.1 1.6 %collective-permute-done.9.rest_3_ = f32[16,128]{1,0:T(8,128)S(1)} collective-permute-done((f32[16,128]{1,0:T(8,128)S(1)}, f32[16,128]{1,0:T(8,128)S(1)}, u32[]{:S(2)}, u32[]{:S(2)}) %collective-permute-start.9) | collective-permute-done | bytes 8224 | tf_op jit(solution)/shard_map/ppermute | solution.py:56
  33.7 0.8 %shard_map.138 = f32[256,128]{1,0:T(8,128)} custom-call(bf16[256,64]{1,0:T(8,128)(2,1)S(1)} %get-tuple-element.49.hot_ref, f32[16,128]{1,0:T(8,128)S(1)} %get-tuple-element.50.rest_0_, f32[16,128]{1,0:T(8,128)S(1)} %collective-permute-done.7.rest_1_, f32[16,128]{1,0:T(8,128)S(1)} %collective-permute-done.8.rest_2_, f32[16,128]{1,0:T(8,128)S(1)} %collective-permute-done.9.rest_3_), custom_call_target="tpu_custom_call" | custom-call | tf_op jit(solution)/shard_map/pallas_call | solution.py:22
  (5 shorter events, 0.0 us)
Async XLA Ops:
  1.7 7.6 %collective-permute-start = (bf16[16,128]{1,0:T(8,128)(2,1)S(1)}, bf16[16,128]{1,0:T(8,128)(2,1)S(1)}, u32[]{:S(2)}, u32[]{:S(2)}) collective-permute-start(bf16[16,128]{1,0:T(8,128)(2,1)S(1)} %get-tuple-element.32), channel_id=1, source_target_pairs={{0,4},{4,0},{8,12},{12,8},{1,5},{5,1},{9,13},{13,9},{2,6},{6,2},{1... | collective-permute-start | bytes 12296 | tf_op jit(solution)/shard_map/ppermute | solution.py:56
  4.8 4.6 %collective-permute-start.1 = (bf16[16,128]{1,0:T(8,128)(2,1)S(1)}, bf16[16,128]{1,0:T(8,128)(2,1)S(1)}, u32[]{:S(2)}, u32[]{:S(2)}) collective-permute-start(bf16[16,128]{1,0:T(8,128)(2,1)S(1)} %get-tuple-element.33), channel_id=1, source_target_pairs={{0,8},{4,12},{8,0},{12,4},{1,9},{5,13},{9,1},{13,5},{2,10},{6,14},... | collective-permute-start | bytes 12296 | tf_op jit(solution)/shard_map/ppermute | solution.py:56
  7.4 5.4 %collective-permute-start.2 = (bf16[16,128]{1,0:T(8,128)(2,1)S(1)}, bf16[16,128]{1,0:T(8,128)(2,1)S(1)}, u32[]{:S(2)}, u32[]{:S(2)}) collective-permute-start(bf16[16,128]{1,0:T(8,128)(2,1)S(1)} %get-tuple-element.34), channel_id=1, source_target_pairs={{0,12},{4,8},{8,4},{12,0},{1,13},{5,9},{9,5},{13,1},{2,14},{6,10},... | collective-permute-start | bytes 12296 | tf_op jit(solution)/shard_map/ppermute | solution.py:56
  13.3 3.8 %collective-permute-start.3 = (bf16[80,128]{1,0:T(8,128)(2,1)S(1)}, bf16[80,128]{1,0:T(8,128)(2,1)S(1)}, u32[]{:S(2)}, u32[]{:S(2)}) collective-permute-start(bf16[80,128]{1,0:T(8,128)(2,1)S(1)} %get-tuple-element.38), channel_id=1, source_target_pairs={{0,4},{4,0},{8,12},{12,8},{1,5},{5,1},{9,13},{13,9},{2,6},{6,2},{1... | collective-permute-start | bytes 61448 | tf_op jit(solution)/shard_map/ppermute | solution.py:49
  13.4 5.6 %collective-permute-start.4 = (bf16[80,128]{1,0:T(8,128)(2,1)S(1)}, bf16[80,128]{1,0:T(8,128)(2,1)S(1)}, u32[]{:S(2)}, u32[]{:S(2)}) collective-permute-start(bf16[80,128]{1,0:T(8,128)(2,1)S(1)} %get-tuple-element.39), channel_id=1, source_target_pairs={{0,12},{4,8},{8,4},{12,0},{1,13},{5,9},{9,5},{13,1},{2,14},{6,10},... | collective-permute-start | bytes 61448 | tf_op jit(solution)/shard_map/ppermute | solution.py:49
  19.2 5.8 %collective-permute-start.6 = (bf16[48,128]{1,0:T(8,128)(2,1)S(1)}, bf16[48,128]{1,0:T(8,128)(2,1)S(1)}, u32[]{:S(2)}, u32[]{:S(2)}) collective-permute-start(bf16[48,128]{1,0:T(8,128)(2,1)S(1)} %get-tuple-element.41), channel_id=1, source_target_pairs={{0,3},{1,2},{2,1},{3,0},{4,7},{5,6},{6,5},{7,4},{8,11},{9,10},{10,... | collective-permute-start | bytes 36872 | tf_op jit(solution)/shard_map/ppermute | solution.py:49
  19.3 5.8 %collective-permute-start.5 = (bf16[48,128]{1,0:T(8,128)(2,1)S(1)}, bf16[48,128]{1,0:T(8,128)(2,1)S(1)}, u32[]{:S(2)}, u32[]{:S(2)}) collective-permute-start(bf16[48,128]{1,0:T(8,128)(2,1)S(1)} %get-tuple-element.41), channel_id=1, source_target_pairs={{0,1},{1,0},{2,3},{3,2},{4,5},{5,4},{6,7},{7,6},{8,9},{9,8},{10,11... | collective-permute-start | bytes 36872 | tf_op jit(solution)/shard_map/ppermute | solution.py:49
  27.1 5.1 %collective-permute-start.7 = (f32[16,128]{1,0:T(8,128)S(1)}, f32[16,128]{1,0:T(8,128)S(1)}, u32[]{:S(2)}, u32[]{:S(2)}) collective-permute-start(f32[16,128]{1,0:T(8,128)S(1)} %get-tuple-element.51), channel_id=1, source_target_pairs={{0,4},{4,0},{8,12},{12,8},{1,5},{5,1},{9,13},{13,9},{2,6},{6,2},{1... | collective-permute-start | bytes 24584 | tf_op jit(solution)/shard_map/ppermute | solution.py:56
  27.2 4.9 %collective-permute-start.8 = (f32[16,128]{1,0:T(8,128)S(1)}, f32[16,128]{1,0:T(8,128)S(1)}, u32[]{:S(2)}, u32[]{:S(2)}) collective-permute-start(f32[16,128]{1,0:T(8,128)S(1)} %get-tuple-element.52), channel_id=1, source_target_pairs={{0,8},{4,12},{8,0},{12,4},{1,9},{5,13},{9,1},{13,5},{2,10},{6,14},... | collective-permute-start | bytes 24584 | tf_op jit(solution)/shard_map/ppermute | solution.py:56
  28.2 5.4 %collective-permute-start.9 = (f32[16,128]{1,0:T(8,128)S(1)}, f32[16,128]{1,0:T(8,128)S(1)}, u32[]{:S(2)}, u32[]{:S(2)}) collective-permute-start(f32[16,128]{1,0:T(8,128)S(1)} %get-tuple-element.53), channel_id=1, source_target_pairs={{0,12},{4,8},{8,4},{12,0},{1,13},{5,9},{9,5},{13,1},{2,14},{6,10},... | collective-permute-start | bytes 24584 | tf_op jit(solution)/shard_map/ppermute | solution.py:56

commit v2 on v1

--- a/solution.py
+++ b/solution.py
@@ -49,11 +49,20 @@
     return lax.ppermute(array_a, axis, first), lax.ppermute(array_b, axis, second)
 
 
+def order(n):
+    return [0] + [k for k in (2, 3, 1) if k < n]
+
+
+def partner(n, split, k):
+    return lax.axis_index("view") ^ order(n)[k] if split else k
+
+
 def exchange(pieces, axis):
     n = lax.axis_size(axis)
     if len(pieces) == 1:
         return [lax.all_to_all(pieces[0], axis, split_axis=0, concat_axis=0, tiled=True)]
-    return [pieces[0]] + [lax.ppermute(pieces[k], axis, [(i, i ^ k) for i in range(n)]) for k in range(1, n)]
+    first, *others = pieces
+    return [first] + [lax.ppermute(p, axis, [(i, i ^ k) for i in range(n)]) for p, k in zip(others, order(n)[1:])]
 
 
 def iota(shape_, dim):
@@ -84,12 +93,11 @@
     outs, (req, cnt, vol, sems) = rest[:-4], rest[-4:]
     copies = fetch([(req_hbm, req), (cnt_hbm, cnt), (vol_hbm, vol)], sems)
     tiles = vol.shape[0]
-    me = lax.axis_index("view")
     copies[0].wait()
     copies[1].wait()
     picks = []
     for k in range(n):
-        column = as_column(wanted_row(req, cnt, me ^ k if split else k))
+        column = as_column(wanted_row(req, cnt, partner(n, split, k)))
         hit = iota((slots, tiles), 1).astype(F32) == column
         picks.append(jnp.where(hit, 1.0, 0.0).astype(BF16))
     copies[2].wait()
@@ -179,8 +187,7 @@
     network_weights(first, second, last, w1_ref, w2_ref, w3_ref)
     for ref, out in ((slopes_1, a1_ref), (slopes_2, a2_ref)):
         out[...] = jnp.broadcast_to(as_column(ref[...]), out.shape)
-    me = lax.axis_index("view")
-    row = jnp.concatenate([wanted_row(req, cnt, me ^ k if split else k) for k in range(n)], axis=1)
+    row = jnp.concatenate([wanted_row(req, cnt, partner(n, split, k)) for k in range(n)], axis=1)
     hit = iota(hot_ref.shape, 0).astype(F32) == row
     hot_ref[...] = jnp.where(hit, 1.0, 0.0).astype(BF16)
     copies[-1].wait()
@@ -193,7 +200,7 @@
     if len(pieces) > 1:
         cap = pieces[0].shape[0]
         for k in range(n):
-            slots_s[pl.ds(pl.multiple_of((me ^ k) * cap, cap), cap), :] = pieces[k][...]
+            slots_s[pl.ds(pl.multiple_of(partner(n, True, k) * cap, cap), cap), :] = pieces[k][...]
         slot_rows = slots_s[...]
     else:
         slot_rows = pieces[0][...]
@@ -282,66 +289,113 @@
     return jnp.maximum(z, slopes * z)
 
 
-def network(inputs, views, w1, w2, w3, a1, a2, s1, s2, s3, update, inside=None):
-    n = s2.shape[2]
+def shifted(z):
+    return pltpu.roll(z, 1, 1), z, pltpu.roll(z, z.shape[1] - 1, 1)
+
+
+def chunks(ref):
+    n = ref.shape[-1]
+    width = min(n, 2 * LANES)
+    return [slice(i, i + width) for i in range(0, n, width)]
+
+
+def first_layer(inputs, count, w1, a1, s1, s2, base=0, inside=None):
     channels = a1.shape[0]
+    for at in chunks(s2):
+        for c in range(3):
+            for b, x in enumerate(shifted(inputs(c, at))):
+                s1[3 * b + c, :, at] = x
+    for k in range(-(-count // BAND)):
+        for at in chunks(s2):
+            m = min(BAND, count - BAND * k) * channels
+            window = jnp.concatenate([s1[j, BAND * k : BAND * k + 16, at] for j in range(9)], axis=0).astype(BF16)
+            z = prelu(jnp.dot(w1[0:m, :], window, preferred_element_type=F32), a1)
+            if inside is not None:
+                z = jnp.where(inside, z, 0.0)
+            row = base + BAND * k * channels
+            for b, x in enumerate(shifted(z)):
+                s2[b, row : row + m, at] = x.astype(BF16)
+
+
+def second_layer(count, w2, a2, s2, s3, base=0, inside=None):
+    channels = a2.shape[0]
+    full = (STEP + 2) * channels
+    for k in range(-(-count // STEP)):
+        part = min(STEP, count - STEP * k)
+        m, depth = part * channels, (part + 2) * channels
+        begin = STEP * k * channels
+        for at in chunks(s2):
+            windows = [s2[b, begin : begin + depth, at] for b in range(3)]
+            if part == STEP:
+                z = jnp.dot(w2[...], jnp.concatenate(windows, axis=0), preferred_element_type=F32)
+            else:
+                z = sum(
+                    jnp.dot(w2[0:m, b * full : b * full + depth], windows[b], preferred_element_type=F32) for b in range(3)
+                )
+            z = prelu(z, a2)
+            if inside is not None:
+                z = jnp.where(inside, z, 0.0)
+            s3[base + begin : base + begin + m, at] = z.astype(BF16)
+
+
+def last_layer(count, channels, w3, s3, update):
+    for k in range(-(-count // STEP)):
+        part = min(STEP, count - STEP * k)
+        begin, depth = STEP * k * channels, (part + 2) * channels
+        for at in chunks(s3):
+            got = jnp.dot(w3[:, 0:depth], s3[begin : begin + depth, at], preferred_element_type=F32)
+            n = got.shape[1]
+            out = pltpu.roll(got[0:8], 1, 1) + got[8:16] + pltpu.roll(got[16:24], n - 1, 1)
+            update[STEP * k : STEP * k + part, at] = out[0:part, :]
+
+
+def inner_kernel(fw_ref, stat_ref, w1, w2, w3, a1, a2, out_ref, one_ref, two_ref, x, s1, s2, s3, update):
+    views = fw_ref.shape[0]
+    channels = a1.shape[0]
+    x[...] = jnp.zeros(x.shape, F32)
     for c in range(3):
-        x = inputs(c)
-        s1[c] = pltpu.roll(x, 1, 1)
-        s1[3 + c] = x
-        s1[6 + c] = pltpu.roll(x, n - 1, 1)
-    total = views + 4
-    for k in range(-(-total // BAND)):
-        m = min(BAND, total - BAND * k) * channels
-        window = jnp.concatenate([s1[j, BAND * k : BAND * k + 16, :] for j in range(9)], axis=0).astype(BF16)
-        z = prelu(jnp.dot(w1[0:m, :], window, preferred_element_type=F32), a1)
-        if inside is not None:
-            z = jnp.where(inside, z, 0.0)
-        at = slice(BAND * k * channels, BAND * k * channels + m)
-        s2[0, at, :] = pltpu.roll(z, 1, 1).astype(BF16)
-        s2[1, at, :] = z.astype(BF16)
-        s2[2, at, :] = pltpu.roll(z, n - 1, 1).astype(BF16)
-    total = views + 2
-    for k in range(-(-total // STEP)):
-        count = min(STEP, total - STEP * k)
-        m, depth = count * channels, (count + 2) * channels
-        begin = STEP * k * channels
-        if count == STEP:
-            window = jnp.concatenate([s2[b, begin : begin + depth, :] for b in range(3)], axis=0)
-            z = jnp.dot(w2[...], window, preferred_element_type=F32)
-        else:
-            full = (STEP + 2) * channels
-            z = sum(
-                jnp.dot(w2[0:m, b * full : b * full + depth], s2[b, begin : begin + depth, :], preferred_element_type=F32)
-                for b in range(3)
-            )
-        z = prelu(z, a2)
-        if inside is not None:
-            z = jnp.where(inside, z, 0.0)
-        s3[begin : begin + m, :] = z.astype(BF16)
-    for k in range(-(-views // STEP)):
-        count = min(STEP, views - STEP * k)
-        depth = (count + 2) * channels
-        begin = STEP * k * channels
-        got = jnp.dot(w3[:, 0:depth], s3[begin : begin + depth, :], preferred_element_type=F32)
-        out = pltpu.roll(got[0:8], 1, 1) + got[8:16] + pltpu.roll(got[16:24], n - 1, 1)
-        update[STEP * k : STEP * k + count, :] = out[0:count, :]
-
-
-def main_kernel(rows, fw_ref, stat_ref, ha_ref, hb_ref, w1, w2, w3, a1, a2, out_ref, x, halo, s1, s2, s3, update):
+        x[c, 0:views, :] = fw_ref[...] if c == 1 else stat_ref[c // 2]
+    first_layer(lambda c, at: x[c, :, at], views - 2, w1, a1, s1, s2)
+    second_layer(views - 4, w2, a2, s2, s3)
+    last_layer(views - 6, channels, w3, s3, update)
+    out_ref[HALO : views - HALO, :] = stat_ref[0, HALO : views - HALO, :] + update[...]
+    two = 2 * channels
+    for ref, ends in ((one_ref, s2.at[1]), (two_ref, s3)):
+        end = ends.shape[0]
+        ref[0:two, :] = ends[0:two, :]
+        ref[two : 2 * two, :] = ends[end - two : end, :]
+
+
+def outer_kernel(
+    fw_ref, stat_ref, ha_ref, hb_ref, in_ref, one_ref, two_ref, w1, w2, w3, a1, a2, out_ref, x, halo, s1, s2, s3, update
+):
     views, wide = fw_ref.shape
+    channels = a1.shape[0]
     sort_halo(ha_ref, hb_ref, halo)
     x[...] = jnp.zeros(x.shape, F32)
     for c in range(3):
-        before, after = halo_of(halo, 0, c, wide), halo_of(halo, 1, c, wide)
-        x[c, 0:HALO, :] = before
-        x[c, HALO : HALO + views, :] = fw_ref[...] if c == 1 else stat_ref[c // 2]
-        x[c, HALO + views : 2 * HALO + views, :] = after
-    cols = fw_ref.shape[1] // rows
-    for r in range(rows):
-        at = slice(r * cols, (r + 1) * cols)
-        network(lambda c: x[c, :, at], views, w1, w2, w3, a1, a2, s1, s2, s3, update)
-        out_ref[:, at] = stat_ref[0, :, at] + update[...]
+        x[0, c, 0:HALO, :] = halo_of(halo, 0, c, wide)
+        x[1, c, 2 : 2 + HALO, :] = halo_of(halo, 1, c, wide)
+        source = fw_ref if c == 1 else stat_ref.at[c // 2]
+        x[0, c, HALO : HALO + 2, :] = source[0:2, :]
+        x[1, c, 0:2, :] = source[views - 2 : views, :]
+    two = 2 * channels
+    new, old = (0, two), (HALO * channels, 0)
+    for side in range(2):
+        kept = slice(side * two, (side + 1) * two)
+        for at in chunks(one_ref):
+            for b, moved in enumerate(shifted(one_ref[kept, at].astype(F32))):
+                s2[side, b, old[side] : old[side] + two, at] = moved.astype(BF16)
+        s3[side, old[side] : old[side] + two, :] = two_ref[kept, :]
+    for side in range(2):
+        first_layer(lambda c, at: x[side, c, :, at], HALO, w1, a1, s1.at[side], s2.at[side], new[side])
+    for side in range(2):
+        second_layer(HALO, w2, a2, s2.at[side], s3.at[side], new[side])
+    for side in range(2):
+        last_layer(HALO, channels, w3, s3.at[side], update.at[side])
+    out_ref[HALO : views - HALO, :] = in_ref[HALO : views - HALO, :]
+    for side, begin in ((0, 0), (1, views - HALO)):
+        out_ref[begin : begin + HALO, :] = stat_ref[0, begin : begin + HALO, :] + update[side]
 
 
 def back_kernel(
@@ -361,7 +415,9 @@
     for c in range(3):
         side = pltpu.roll(sides, (-HALO * c) % LANES, 1)
         x[c] = jnp.where(from_left | from_right, side, strip_ref[c])
-    network(lambda c: x[c], views, w1, w2, w3, a1, a2, s1, s2, s3, update, inside)
+    first_layer(lambda c, at: x[c, :, at], views + 4, w1, a1, s1, s2, 0, inside)
+    second_layer(views + 2, w2, a2, s2, s3, 0, inside)
+    last_layer(views, a1.shape[0], w3, s3, update)
     strip = x[0, HALO : HALO + views, :] + update[...]
     first = iota((views, LANES), 1)
     for r in range(rows):
@@ -391,9 +447,8 @@
     if len(parts) > 1:
         part_s[...] = partial
         cap = parts[0].shape[0]
-        group = lax.axis_index("view")
         for k in range(n):
-            parts[k][...] = part_s[pl.ds(pl.multiple_of((group ^ k) * cap, cap), cap), :]
+            parts[k][...] = part_s[pl.ds(pl.multiple_of(partner(n, True, k) * cap, cap), cap), :]
     else:
         parts[0][...] = partial
 
@@ -497,20 +552,30 @@
     )
     side_a, side_b = both_ways(message, message, "col")
 
-    def net_scratch(width):
+    def net_scratch(count, width, one=None, *lead):
+        one = one or count + 4
         return [
-            pltpu.VMEM((9, padded, width), F32),
-            pltpu.VMEM((3, (views + 4) * channels, width), BF16),
-            pltpu.VMEM(((views + 2) * channels, width), BF16),
-            pltpu.VMEM((views, width), F32),
+            pltpu.VMEM((*lead, 9, -(-one // BAND) * BAND + BAND, width), F32),
+            pltpu.VMEM((*lead, 3, (count + 4) * channels, width), BF16),
+            pltpu.VMEM((*lead, (count + 2) * channels, width), BF16),
+            pltpu.VMEM((*lead, count, width), F32),
         ]
 
+    weights = [w1, w2, w3, a1, a2]
+    ends = shape((4 * channels, wide), BF16)
+    inner, one, two = call(
+        inner_kernel,
+        [shape((views, wide)), ends, ends],
+        [pltpu.VMEM((3, views + BAND, wide), F32), *net_scratch(views - 2 * HALO, wide)],
+        [fw, stat, *weights],
+        cost=(2 * 10**9, 4 * 10**6),
+    )
     main = call(
-        functools.partial(main_kernel, rows),
+        outer_kernel,
         shape((views, wide)),
-        [pltpu.VMEM((3, padded, wide), F32), halo, *net_scratch(cols)],
-        [fw, stat, halo_a, halo_b, w1, w2, w3, a1, a2],
-        cost=(2 * 10**9, 4 * 10**6),
+        [pltpu.VMEM((2, 3, 2 * BAND, wide), F32), halo, *net_scratch(HALO, wide, HALO, 2)],
+        [fw, stat, halo_a, halo_b, inner, one, two, *weights],
+        cost=(4 * 10**8, 2 * 10**6),
     )
     parts = [shape((slots, vox))] * n if split else [shape((n * slots, vox))]
     dual_out, *returned = call(
@@ -518,12 +583,12 @@
         [shape((views * rows, cols), BF16), *parts],
         [
             pltpu.VMEM((3, padded, LANES), F32),
-            *net_scratch(LANES),
+            *net_scratch(views, LANES),
             flat,
             pltpu.VMEM((views * rows, vox), BF16),
             pltpu.VMEM((n * slots, vox), F32),
         ],
-        [strip, side_a, side_b, w1, w2, w3, a1, a2, main, foot, axial_back],
+        [strip, side_a, side_b, *weights, main, foot, axial_back],
     )
     arrived = exchange(returned, "view")
     backprojection = call(scatter_kernel, shape((tiles, vox)), [], [hot, *arrived])

time: 34.7 us -> 31 us (0.89)
  waiting for transfers between devices: 9.82 us -> 4.62 us
  starting transfers between devices: 12.3 us -> 13.6 us
    ppermute x2, starting transfers between devices: 0.59 us -> 4.29 us  [both_ways(): lax.ppermute(array_b, axis, second)]
    ppermute x2, waiting for transfers between devices: 2.94 us -> 0.01 us  [both_ways(): lax.ppermute(array_a, axis, first)]
    ppermute x2, starting transfers between devices: 1.66 us -> 0.1 us  [both_ways(): lax.ppermute(array_a, axis, first)]
    ppermute x2, waiting for transfers between devices: 1.88 us -> 0.44 us  [both_ways(): lax.ppermute(array_b, axis, second)]
    ppermute x6, starting transfers between devices: 10.1 us -> 9.19 us  [exchange(): lax.ppermute(p, axis, [(i, i ^ k) for i in range(n)])]
    ppermute x6, waiting for transfers between devices: 5 us -> 4.18 us  [exchange(): lax.ppermute(p, axis, [(i, i ^ k) for i in range(n)])]
    pallas_call x8 -> x9, Pallas kernels: 11 us -> 11.3 us  [call(): pl.pallas_call(body, out_shape=outs if single else list(outs), in_specs=s...]
  transfers between devices with their start and end apart: 10 -> 10, of which waited for: 4 -> 5; matrix products, arithmetic and copies ran while one was open for 2% -> 2% of each run, Pallas kernels for 18% -> 22%
where the time goes in v2:
time: 31 us; the launch traced here: 30.8 us
  starting transfers between devices  13.6 us (44%)
  Pallas kernels  11.3 us (36%)
  waiting for transfers between devices  4.62 us (15%)
  between operations  0.73 us (2%)
  local copies, waits for them, and re-layouts  0.65 us (2%)
    pallas_call x9, Pallas kernels, call(): pl.pallas_call(body, out_shape=outs if single else list(outs), in_specs=s...  11.3 us
    ppermute x6, starting transfers between devices, exchange(): lax.ppermute(p, axis, [(i, i ^ k) for i in range(n)])  9.19 us
    ppermute x2, starting transfers between devices, both_ways(): lax.ppermute(array_b, axis, second)  4.29 us
    ppermute x6, waiting for transfers between devices, exchange(): lax.ppermute(p, axis, [(i, i ^ k) for i in range(n)])  4.18 us
    reshape x1, local copies, waits for them, and re-layouts, shards(): return (dual_out.reshape(views, rows, cols), backprojection)  0.65 us
  transfers between devices with their start and end apart: 10, of which 5 were waited for; matrix products, arithmetic and copies ran while one was open for 2% of the time, Pallas kernels for 22%

profile of v2, /device:TPU:0, one launch (start us, length us, event | category | flops | bytes accessed | tf_op | source)
XLA Modules:
  0.0 30.8 jit_solution(8900042561344279711)
XLA Ops:
  0.6 1.1 %shard_map.132 = (bf16[16,128]{1,0:T(8,128)(2,1)S(1)}, bf16[16,128]{1,0:T(8,128)(2,1)S(1)}, bf16[16,128]{1,0:T(8,128)(2,1)S(1)}, bf16[16,128]{1,0:T(8,128)(2,1)S(1)}) custom-call(s32[1,4,16]{2,1,0:T(4,128)} %req_hbm.1, s32[1,4]{1,0:T(1,128)} %cnt_hbm.1, bf16[256,128]{1,0:T(8,128)(2,1)} %vol_hbm.1), custom_call_target="tpu_custom_call" | custom-call | tf_op jit(solution)/shard_map/pallas_call | solution.py:22
  1.7 4.1 %collective-permute-start = (bf16[16,128]{1,0:T(8,128)(2,1)S(1)}, bf16[16,128]{1,0:T(8,128)(2,1)S(1)}, u32[]{:S(2)}, u32[]{:S(2)}) collective-permute-start(bf16[16,128]{1,0:T(8,128)(2,1)S(1)} %get-tuple-element.35), channel_id=1, source_target_pairs={{0,8},{4,12},{8,0},{12,4},{1,9},{5,13},{9,1},{13,5},{2,10},{6,14},... | collective-permute-start | bytes 12296 | tf_op jit(solution)/shard_map/ppermute | solution.py:65
  5.8 1.3 %collective-permute-start.1 = (bf16[16,128]{1,0:T(8,128)(2,1)S(1)}, bf16[16,128]{1,0:T(8,128)(2,1)S(1)}, u32[]{:S(2)}, u32[]{:S(2)}) collective-permute-start(bf16[16,128]{1,0:T(8,128)(2,1)S(1)} %get-tuple-element.36), channel_id=1, source_target_pairs={{0,12},{4,8},{8,4},{12,0},{1,13},{5,9},{9,5},{13,1},{2,14},{6,10},... | collective-permute-start | bytes 12296 | tf_op jit(solution)/shard_map/ppermute | solution.py:65
  7.1 0.2 collective-permute-start.2
  7.4 2.0 %shard_map.131 = (f32[2,32,1024]{2,1,0:T(8,128)S(1)}, bf16[32,128,256]{2,1,0:T(8,128)(2,1)S(1)}, bf16[128,64]{1,0:T(8,128)(2,1)S(1)}, bf16[64,128]{1,0:T(8,128)(...) custom-call(bf16[32,4,256]{2,1,0:T(4,128)(2,1)} %refs_0_.1, ...), custom_call_target="tpu_custom_call" | custom-call | flops 100000000 | bytes 4000000 | tf_op jit(solution)/shard_map/pallas_call | solution.py:22
  9.3 1.9 %collective-permute-done.1.rest_2_ = bf16[16,128]{1,0:T(8,128)(2,1)S(1)} collective-permute-done((bf16[16,128]{1,0:T(8,128)(2,1)S(1)}, bf16[16,128]{1,0:T(8,128)(2,1)S(1)}, u32[]{:S(2)}, u32[]{:S(2)}) %collective-permute-start.1) | collective-permute-done | bytes 4128 | tf_op jit(solution)/shard_map/ppermute | solution.py:65
  11.2 0.5 %shard_map.133 = (f32[32,1024]{1,0:T(8,128)S(1)}, bf16[80,128]{1,0:T(8,128)(2,1)S(1)}, bf16[80,128]{1,0:T(8,128)(2,1)S(1)}) custom-call(bf16[128,64]{1,0:T(8,128)(2,1)S(1)} %get-tuple-element.31.axial_ref, bf16[32,128,256]{2,1,0:T(8,128)(2,1)S(1)} %get-tuple-element.32.foot_ref, f32[2,32,1024]{2,1,0:T(8,128)S(1)} %get-tuple-element.33.stat_ref, ...), custom_call_target="tpu_custom_call" | custom-call | tf_op jit(solution)/shard_map/pallas_call | solution.py:22
  11.7 0.1 collective-permute-start.3
  11.8 2.7 %collective-permute-start.4 = (bf16[80,128]{1,0:T(8,128)(2,1)S(1)}, bf16[80,128]{1,0:T(8,128)(2,1)S(1)}, u32[]{:S(2)}, u32[]{:S(2)}) collective-permute-start(bf16[80,128]{1,0:T(8,128)(2,1)S(1)} %get-tuple-element.42), channel_id=1, source_target_pairs={{0,12},{4,8},{8,4},{12,0},{1,13},{5,9},{9,5},{13,1},{2,14},{6,10},... | collective-permute-start | bytes 61448 | tf_op jit(solution)/shard_map/ppermute | solution.py:49
  14.5 3.3 %shard_map.136 = (f32[32,1024]{1,0:T(8,128)S(1)}, bf16[128,1024]{1,0:T(8,128)(2,1)S(1)}, bf16[128,1024]{1,0:T(8,128)(2,1)S(1)}) custom-call(f32[32,1024]{1,0:T(8,128)S(1)} %get-tuple-element.38.fw_ref, f32[2,32,1024]{2,1,0:T(8,128)S(1)} %get-tuple-element.33.stat_ref, bf16[256,144]{1,0:T(8,128)(2,1)S(1)} %get-tuple-element.45.w1, ...), custom_call_target="tpu_custom_call" | custom-call | flops 2000000000 | bytes 4000000 | tf_op jit(solution)/shard_map/pallas_call | solution.py:22
  17.8 0.3 shard_map.134
  18.1 0.2 shard_map.135
  18.3 1.6 %collective-permute-start.6 = (bf16[48,128]{1,0:T(8,128)(2,1)S(1)}, bf16[48,128]{1,0:T(8,128)(2,1)S(1)}, u32[]{:S(2)}, u32[]{:S(2)}) collective-permute-start(bf16[48,128]{1,0:T(8,128)(2,1)S(1)} %get-tuple-element.44), channel_id=1, source_target_pairs={{0,3},{1,2},{2,1},{3,0},{4,7},{5,6},{6,5},{7,4},{8,11},{9,10},{10,... | collective-permute-start | bytes 36872 | tf_op jit(solution)/shard_map/ppermute | solution.py:49
  19.9 1.1 %shard_map.137.main_ref = f32[32,1024]{1,0:T(8,128)S(1)} custom-call(f32[32,1024]{1,0:T(8,128)S(1)} %get-tuple-element.38.fw_ref, f32[2,32,1024]{2,1,0:T(8,128)S(1)} %get-tuple-element.33.stat_ref, bf16[80,128]{1,0:T(8,128)(2,1)S(1)} %collective-permute-done.3.a_ref.ha_ref, bf16[80,128]{1,0:T(8,128)(2,1)S(1)} %collective-permute-done.4.b_ref.hb_ref, ...), custom_call_target="tpu_custom_call" | custom-call | flops 400000000 | bytes 2000000 | tf_op jit(solution)/shard_map/pallas_call | solution.py:22
  21.1 0.4 %collective-permute-done.6.rb_ref = bf16[48,128]{1,0:T(8,128)(2,1)S(1)} collective-permute-done((bf16[48,128]{1,0:T(8,128)(2,1)S(1)}, bf16[48,128]{1,0:T(8,128)(2,1)S(1)}, u32[]{:S(2)}, u32[]{:S(2)}) %collective-permute-start.6) | collective-permute-done | bytes 12320 | tf_op jit(solution)/shard_map/ppermute | solution.py:49
  21.5 2.0 %shard_map.138 = (bf16[128,256]{1,0:T(8,128)(2,1)S(1)}, f32[16,128]{1,0:T(8,128)S(1)}, f32[16,128]{1,0:T(8,128)S(1)}, f32[16,128]{1,0:T(8,128)S(1)}, f32[16,128]{1,0:T(8,128)S(1)}) custom-call(f32[3,48,128]{2,1,0:T(8,128)S(1)} %get-tuple-element.43.strip_ref, bf16[48,128]{1,0:T(8,128)(2,1)S(1)} %collective-permute-done.5.ra_ref, ...), custom_call_target="tpu_custom_call" | custom-call | tf_op jit(solution)/shard_map/pallas_call | solution.py:22
  23.5 0.8 %collective-permute-start.7 = (f32[16,128]{1,0:T(8,128)S(1)}, f32[16,128]{1,0:T(8,128)S(1)}, u32[]{:S(2)}, u32[]{:S(2)}) collective-permute-start(f32[16,128]{1,0:T(8,128)S(1)} %get-tuple-element.57), channel_id=1, source_target_pairs={{0,8},{4,12},{8,0},{12,4},{1,9},{5,13},{9,1},{13,5},{2,10},{6,14},... | collective-permute-start | bytes 24584 | tf_op jit(solution)/shard_map/ppermute | solution.py:65
  24.3 2.0 %collective-permute-start.8 = (f32[16,128]{1,0:T(8,128)S(1)}, f32[16,128]{1,0:T(8,128)S(1)}, u32[]{:S(2)}, u32[]{:S(2)}) collective-permute-start(f32[16,128]{1,0:T(8,128)S(1)} %get-tuple-element.58), channel_id=1, source_target_pairs={{0,12},{4,8},{8,4},{12,0},{1,13},{5,9},{9,5},{13,1},{2,14},{6,10},... | collective-permute-start | bytes 24584 | tf_op jit(solution)/shard_map/ppermute | solution.py:65
  26.3 0.7 %collective-permute-start.9 = (f32[16,128]{1,0:T(8,128)S(1)}, f32[16,128]{1,0:T(8,128)S(1)}, u32[]{:S(2)}, u32[]{:S(2)}) collective-permute-start(f32[16,128]{1,0:T(8,128)S(1)} %get-tuple-element.59), channel_id=1, source_target_pairs={{0,4},{4,0},{8,12},{12,8},{1,5},{5,1},{9,13},{13,9},{2,6},{6,2},{1... | collective-permute-start | bytes 24584 | tf_op jit(solution)/shard_map/ppermute | solution.py:65
  27.0 0.6 %reshape.19 = bf16[32,4,256]{2,1,0:T(4,128)(2,1)} reshape(bf16[128,256]{1,0:T(8,128)(2,1)S(1)} %get-tuple-element.54) | data formatting | bytes 131072 | tf_op jit(solution)/shard_map/reshape | solution.py:595
  27.7 0.4 %collective-permute-done.7.rest_1_ = f32[16,128]{1,0:T(8,128)S(1)} collective-permute-done((f32[16,128]{1,0:T(8,128)S(1)}, f32[16,128]{1,0:T(8,128)S(1)}, u32[]{:S(2)}, u32[]{:S(2)}) %collective-permute-start.7) | collective-permute-done | bytes 8224 | tf_op jit(solution)/shard_map/ppermute | solution.py:65
  28.1 1.7 %collective-permute-done.8.rest_2_ = f32[16,128]{1,0:T(8,128)S(1)} collective-permute-done((f32[16,128]{1,0:T(8,128)S(1)}, f32[16,128]{1,0:T(8,128)S(1)}, u32[]{:S(2)}, u32[]{:S(2)}) %collective-permute-start.8) | collective-permute-done | bytes 8224 | tf_op jit(solution)/shard_map/ppermute | solution.py:65
  29.8 0.2 collective-permute-done.9.rest_3_
  30.0 0.8 %shard_map.139 = f32[256,128]{1,0:T(8,128)} custom-call(bf16[256,64]{1,0:T(8,128)(2,1)S(1)} %get-tuple-element.55.hot_ref, f32[16,128]{1,0:T(8,128)S(1)} %get-tuple-element.56.rest_0_, f32[16,128]{1,0:T(8,128)S(1)} %collective-permute-done.7.rest_1_, f32[16,128]{1,0:T(8,128)S(1)} %collective-permute-done.8.rest_2_, f32[16,128]{1,0:T(8,128)S(1)} %collective-permute-done.9.rest_3_), custom_call_target="tpu_custom_call" | custom-call | tf_op jit(solution)/shard_map/pallas_call | solution.py:22
  (6 shorter events, 0.0 us)
Async XLA Ops:
  1.7 7.6 %collective-permute-start = (bf16[16,128]{1,0:T(8,128)(2,1)S(1)}, bf16[16,128]{1,0:T(8,128)(2,1)S(1)}, u32[]{:S(2)}, u32[]{:S(2)}) collective-permute-start(bf16[16,128]{1,0:T(8,128)(2,1)S(1)} %get-tuple-element.35), channel_id=1, source_target_pairs={{0,8},{4,12},{8,0},{12,4},{1,9},{5,13},{9,1},{13,5},{2,10},{6,14},... | collective-permute-start | bytes 12296 | tf_op jit(solution)/shard_map/ppermute | solution.py:65
  5.8 5.4 %collective-permute-start.1 = (bf16[16,128]{1,0:T(8,128)(2,1)S(1)}, bf16[16,128]{1,0:T(8,128)(2,1)S(1)}, u32[]{:S(2)}, u32[]{:S(2)}) collective-permute-start(bf16[16,128]{1,0:T(8,128)(2,1)S(1)} %get-tuple-element.36), channel_id=1, source_target_pairs={{0,12},{4,8},{8,4},{12,0},{1,13},{5,9},{9,5},{13,1},{2,14},{6,10},... | collective-permute-start | bytes 12296 | tf_op jit(solution)/shard_map/ppermute | solution.py:65
  7.1 4.1 %collective-permute-start.2 = (bf16[16,128]{1,0:T(8,128)(2,1)S(1)}, bf16[16,128]{1,0:T(8,128)(2,1)S(1)}, u32[]{:S(2)}, u32[]{:S(2)}) collective-permute-start(bf16[16,128]{1,0:T(8,128)(2,1)S(1)} %get-tuple-element.37), channel_id=1, source_target_pairs={{0,4},{4,0},{8,12},{12,8},{1,5},{5,1},{9,13},{13,9},{2,6},{6,2},{1... | collective-permute-start | bytes 12296 | tf_op jit(solution)/shard_map/ppermute | solution.py:65
  11.7 6.3 %collective-permute-start.3 = (bf16[80,128]{1,0:T(8,128)(2,1)S(1)}, bf16[80,128]{1,0:T(8,128)(2,1)S(1)}, u32[]{:S(2)}, u32[]{:S(2)}) collective-permute-start(bf16[80,128]{1,0:T(8,128)(2,1)S(1)} %get-tuple-element.41), channel_id=1, source_target_pairs={{0,4},{4,0},{8,12},{12,8},{1,5},{5,1},{9,13},{13,9},{2,6},{6,2},{1... | collective-permute-start | bytes 61448 | tf_op jit(solution)/shard_map/ppermute | solution.py:49
  11.8 6.3 %collective-permute-start.4 = (bf16[80,128]{1,0:T(8,128)(2,1)S(1)}, bf16[80,128]{1,0:T(8,128)(2,1)S(1)}, u32[]{:S(2)}, u32[]{:S(2)}) collective-permute-start(bf16[80,128]{1,0:T(8,128)(2,1)S(1)} %get-tuple-element.42), channel_id=1, source_target_pairs={{0,12},{4,8},{8,4},{12,0},{1,13},{5,9},{9,5},{13,1},{2,14},{6,10},... | collective-permute-start | bytes 61448 | tf_op jit(solution)/shard_map/ppermute | solution.py:49
  18.3 2.8 %collective-permute-start.5 = (bf16[48,128]{1,0:T(8,128)(2,1)S(1)}, bf16[48,128]{1,0:T(8,128)(2,1)S(1)}, u32[]{:S(2)}, u32[]{:S(2)}) collective-permute-start(bf16[48,128]{1,0:T(8,128)(2,1)S(1)} %get-tuple-element.44), channel_id=1, source_target_pairs={{0,1},{1,0},{2,3},{3,2},{4,5},{5,4},{6,7},{7,6},{8,9},{9,8},{10,11... | collective-permute-start | bytes 36872 | tf_op jit(solution)/shard_map/ppermute | solution.py:49
  18.3 3.2 %collective-permute-start.6 = (bf16[48,128]{1,0:T(8,128)(2,1)S(1)}, bf16[48,128]{1,0:T(8,128)(2,1)S(1)}, u32[]{:S(2)}, u32[]{:S(2)}) collective-permute-start(bf16[48,128]{1,0:T(8,128)(2,1)S(1)} %get-tuple-element.44), channel_id=1, source_target_pairs={{0,3},{1,2},{2,1},{3,0},{4,7},{5,6},{6,5},{7,4},{8,11},{9,10},{10,... | collective-permute-start | bytes 36872 | tf_op jit(solution)/shard_map/ppermute | solution.py:49
  23.5 4.6 %collective-permute-start.7 = (f32[16,128]{1,0:T(8,128)S(1)}, f32[16,128]{1,0:T(8,128)S(1)}, u32[]{:S(2)}, u32[]{:S(2)}) collective-permute-start(f32[16,128]{1,0:T(8,128)S(1)} %get-tuple-element.57), channel_id=1, source_target_pairs={{0,8},{4,12},{8,0},{12,4},{1,9},{5,13},{9,1},{13,5},{2,10},{6,14},... | collective-permute-start | bytes 24584 | tf_op jit(solution)/shard_map/ppermute | solution.py:65
  24.3 5.4 %collective-permute-start.8 = (f32[16,128]{1,0:T(8,128)S(1)}, f32[16,128]{1,0:T(8,128)S(1)}, u32[]{:S(2)}, u32[]{:S(2)}) collective-permute-start(f32[16,128]{1,0:T(8,128)S(1)} %get-tuple-element.58), channel_id=1, source_target_pairs={{0,12},{4,8},{8,4},{12,0},{1,13},{5,9},{9,5},{13,1},{2,14},{6,10},... | collective-permute-start | bytes 24584 | tf_op jit(solution)/shard_map/ppermute | solution.py:65
  26.3 3.7 %collective-permute-start.9 = (f32[16,128]{1,0:T(8,128)S(1)}, f32[16,128]{1,0:T(8,128)S(1)}, u32[]{:S(2)}, u32[]{:S(2)}) collective-permute-start(f32[16,128]{1,0:T(8,128)S(1)} %get-tuple-element.59), channel_id=1, source_target_pairs={{0,4},{4,0},{8,12},{12,8},{1,5},{5,1},{9,13},{13,9},{2,6},{6,2},{1... | collective-permute-start | bytes 24584 | tf_op jit(solution)/shard_map/ppermute | solution.py:65

commit v3 on v2

--- a/solution.py
+++ b/solution.py
@@ -101,12 +101,12 @@
         hit = iota((slots, tiles), 1).astype(F32) == column
         picks.append(jnp.where(hit, 1.0, 0.0).astype(BF16))
     copies[2].wait()
-    for k in range(n):
-        got = jnp.dot(picks[k], vol[...], preferred_element_type=F32).astype(BF16)
-        if split:
-            outs[k][...] = got
-        else:
-            outs[0][k * slots : (k + 1) * slots, :] = got
+    got = jnp.dot(jnp.concatenate(picks, axis=0), vol[...], preferred_element_type=F32).astype(BF16)
+    if split:
+        for k in range(n):
+            outs[k][...] = got[k * slots : (k + 1) * slots, :]
+    else:
+        outs[0][...] = got
 
 
 def scatter_kernel(hot_ref, *rest):
@@ -313,8 +313,8 @@
             if inside is not None:
                 z = jnp.where(inside, z, 0.0)
             row = base + BAND * k * channels
-            for b, x in enumerate(shifted(z)):
-                s2[b, row : row + m, at] = x.astype(BF16)
+            for b, x in enumerate(shifted(z.astype(BF16))):
+                s2[b, row : row + m, at] = x
 
 
 def second_layer(count, w2, a2, s2, s3, base=0, inside=None):
@@ -384,8 +384,8 @@
     for side in range(2):
         kept = slice(side * two, (side + 1) * two)
         for at in chunks(one_ref):
-            for b, moved in enumerate(shifted(one_ref[kept, at].astype(F32))):
-                s2[side, b, old[side] : old[side] + two, at] = moved.astype(BF16)
+            for b, moved in enumerate(shifted(one_ref[kept, at])):
+                s2[side, b, old[side] : old[side] + two, at] = moved
         s3[side, old[side] : old[side] + two, :] = two_ref[kept, :]
     for side in range(2):
         first_layer(lambda c, at: x[side, c, :, at], HALO, w1, a1, s1.at[side], s2.at[side], new[side])
@@ -412,13 +412,18 @@
     inside = (left_side & ((step >= HALO) | (me > 0))) | ((~left_side) & ((step < 6) | (me < peers - 1)))
     a, b = ra_ref[...].astype(F32), rb_ref[...].astype(F32)
     sides = jnp.where(at < 64, jnp.where(even, b, a), jnp.where(even, a, b))
+    half = views // 2
     for c in range(3):
         side = pltpu.roll(sides, (-HALO * c) % LANES, 1)
-        x[c] = jnp.where(from_left | from_right, side, strip_ref[c])
-    first_layer(lambda c, at: x[c, :, at], views + 4, w1, a1, s1, s2, 0, inside)
-    second_layer(views + 2, w2, a2, s2, s3, 0, inside)
-    last_layer(views, a1.shape[0], w3, s3, update)
-    strip = x[0, HALO : HALO + views, :] + update[...]
+        joined = jnp.where(from_left | from_right, side, strip_ref[c])
+        x[c, :, 0:LANES] = joined[0 : x.shape[1], :]
+        x[c, :, LANES:] = joined[half : half + x.shape[1], :]
+    inside = jnp.concatenate([inside, inside], axis=1)
+    first_layer(lambda c, at: x[c, :, at], half + 4, w1, a1, s1, s2, 0, inside)
+    second_layer(half + 2, w2, a2, s2, s3, 0, inside)
+    last_layer(half, a1.shape[0], w3, s3, update)
+    strip = x[0, HALO : HALO + half, :] + update[...]
+    strip = jnp.concatenate([strip[:, 0:LANES], strip[:, LANES:]], axis=0)
     first = iota((views, LANES), 1)
     for r in range(rows):
         head = main_ref[:, r * cols : r * cols + LANES]
@@ -582,8 +587,8 @@
         functools.partial(back_kernel, n, rows),
         [shape((views * rows, cols), BF16), *parts],
         [
-            pltpu.VMEM((3, padded, LANES), F32),
-            *net_scratch(views, LANES),
+            pltpu.VMEM((3, padded - views // 2, 2 * LANES), F32),
+            *net_scratch(views // 2, 2 * LANES),
             flat,
             pltpu.VMEM((views * rows, vox), BF16),
             pltpu.VMEM((n * slots, vox), F32),

time: 31 us -> 30.4 us (0.981)
  Pallas kernels: 11.3 us -> 10.5 us
    pallas_call x9, Pallas kernels: 11.3 us -> 10.5 us  [call(): pl.pallas_call(body, out_shape=outs if single else list(outs), in_specs=s...]
  transfers between devices with their start and end apart: 10 -> 10, of which waited for: 5 -> 5; matrix products, arithmetic and copies ran while one was open for 2% -> 2% of each run, Pallas kernels for 22% -> 20%
where the time goes in v3:
time: 30.4 us; the launch traced here: 30.2 us
  starting transfers between devices  13.6 us (45%)
  Pallas kernels  10.5 us (35%)
  waiting for transfers between devices  4.73 us (16%)
  between operations  0.73 us (2%)
  local copies, waits for them, and re-layouts  0.65 us (2%)
    pallas_call x9, Pallas kernels, call(): pl.pallas_call(body, out_shape=outs if single else list(outs), in_specs=s...  10.5 us
    ppermute x6, starting transfers between devices, exchange(): lax.ppermute(p, axis, [(i, i ^ k) for i in range(n)])  9.19 us
    ppermute x2, starting transfers between devices, both_ways(): lax.ppermute(array_b, axis, second)  4.29 us
    ppermute x6, waiting for transfers between devices, exchange(): lax.ppermute(p, axis, [(i, i ^ k) for i in range(n)])  4.18 us
    reshape x1, local copies, waits for them, and re-layouts, shards(): return (dual_out.reshape(views, rows, cols), backprojection)  0.65 us
  transfers between devices with their start and end apart: 10, of which 5 were waited for; matrix products, arithmetic and copies ran while one was open for 2% of the time, Pallas kernels for 20%

profile of v3, /device:TPU:0, one launch (start us, length us, event | category | flops | bytes accessed | tf_op | source)
XLA Modules:
  0.0 30.2 jit_solution(3391391121643277014)
XLA Ops:
  0.6 1.0 %shard_map.132 = (bf16[16,128]{1,0:T(8,128)(2,1)S(1)}, bf16[16,128]{1,0:T(8,128)(2,1)S(1)}, bf16[16,128]{1,0:T(8,128)(2,1)S(1)}, bf16[16,128]{1,0:T(8,128)(2,1)S(1)}) custom-call(s32[1,4,16]{2,1,0:T(4,128)} %req_hbm.1, s32[1,4]{1,0:T(1,128)} %cnt_hbm.1, bf16[256,128]{1,0:T(8,128)(2,1)} %vol_hbm.1), custom_call_target="tpu_custom_call" | custom-call | tf_op jit(solution)/shard_map/pallas_call | solution.py:22
  1.7 4.1 %collective-permute-start = (bf16[16,128]{1,0:T(8,128)(2,1)S(1)}, bf16[16,128]{1,0:T(8,128)(2,1)S(1)}, u32[]{:S(2)}, u32[]{:S(2)}) collective-permute-start(bf16[16,128]{1,0:T(8,128)(2,1)S(1)} %get-tuple-element.35), channel_id=1, source_target_pairs={{0,8},{4,12},{8,0},{12,4},{1,9},{5,13},{9,1},{13,5},{2,10},{6,14},... | collective-permute-start | bytes 12296 | tf_op jit(solution)/shard_map/ppermute | solution.py:65
  5.8 1.3 %collective-permute-start.1 = (bf16[16,128]{1,0:T(8,128)(2,1)S(1)}, bf16[16,128]{1,0:T(8,128)(2,1)S(1)}, u32[]{:S(2)}, u32[]{:S(2)}) collective-permute-start(bf16[16,128]{1,0:T(8,128)(2,1)S(1)} %get-tuple-element.36), channel_id=1, source_target_pairs={{0,12},{4,8},{8,4},{12,0},{1,13},{5,9},{9,5},{13,1},{2,14},{6,10},... | collective-permute-start | bytes 12296 | tf_op jit(solution)/shard_map/ppermute | solution.py:65
  7.1 0.2 collective-permute-start.2
  7.4 2.0 %shard_map.131 = (f32[2,32,1024]{2,1,0:T(8,128)S(1)}, bf16[32,128,256]{2,1,0:T(8,128)(2,1)S(1)}, bf16[128,64]{1,0:T(8,128)(2,1)S(1)}, bf16[64,128]{1,0:T(8,128)(...) custom-call(bf16[32,4,256]{2,1,0:T(4,128)(2,1)} %refs_0_.1, ...), custom_call_target="tpu_custom_call" | custom-call | flops 100000000 | bytes 4000000 | tf_op jit(solution)/shard_map/pallas_call | solution.py:22
  9.3 1.9 %collective-permute-done.1.rest_2_ = bf16[16,128]{1,0:T(8,128)(2,1)S(1)} collective-permute-done((bf16[16,128]{1,0:T(8,128)(2,1)S(1)}, bf16[16,128]{1,0:T(8,128)(2,1)S(1)}, u32[]{:S(2)}, u32[]{:S(2)}) %collective-permute-start.1) | collective-permute-done | bytes 4128 | tf_op jit(solution)/shard_map/ppermute | solution.py:65
  11.2 0.5 %shard_map.133 = (f32[32,1024]{1,0:T(8,128)S(1)}, bf16[80,128]{1,0:T(8,128)(2,1)S(1)}, bf16[80,128]{1,0:T(8,128)(2,1)S(1)}) custom-call(bf16[128,64]{1,0:T(8,128)(2,1)S(1)} %get-tuple-element.31.axial_ref, bf16[32,128,256]{2,1,0:T(8,128)(2,1)S(1)} %get-tuple-element.32.foot_ref, f32[2,32,1024]{2,1,0:T(8,128)S(1)} %get-tuple-element.33.stat_ref, ...), custom_call_target="tpu_custom_call" | custom-call | tf_op jit(solution)/shard_map/pallas_call | solution.py:22
  11.7 0.1 collective-permute-start.3
  11.8 2.7 %collective-permute-start.4 = (bf16[80,128]{1,0:T(8,128)(2,1)S(1)}, bf16[80,128]{1,0:T(8,128)(2,1)S(1)}, u32[]{:S(2)}, u32[]{:S(2)}) collective-permute-start(bf16[80,128]{1,0:T(8,128)(2,1)S(1)} %get-tuple-element.42), channel_id=1, source_target_pairs={{0,12},{4,8},{8,4},{12,0},{1,13},{5,9},{9,5},{13,1},{2,14},{6,10},... | collective-permute-start | bytes 61448 | tf_op jit(solution)/shard_map/ppermute | solution.py:49
  14.5 2.8 %shard_map.136 = (f32[32,1024]{1,0:T(8,128)S(1)}, bf16[128,1024]{1,0:T(8,128)(2,1)S(1)}, bf16[128,1024]{1,0:T(8,128)(2,1)S(1)}) custom-call(f32[32,1024]{1,0:T(8,128)S(1)} %get-tuple-element.38.fw_ref, f32[2,32,1024]{2,1,0:T(8,128)S(1)} %get-tuple-element.33.stat_ref, bf16[256,144]{1,0:T(8,128)(2,1)S(1)} %get-tuple-element.45.w1, ...), custom_call_target="tpu_custom_call" | custom-call | flops 2000000000 | bytes 4000000 | tf_op jit(solution)/shard_map/pallas_call | solution.py:22
  17.3 0.3 shard_map.134
  17.6 0.2 shard_map.135
  17.8 1.6 %collective-permute-start.6 = (bf16[48,128]{1,0:T(8,128)(2,1)S(1)}, bf16[48,128]{1,0:T(8,128)(2,1)S(1)}, u32[]{:S(2)}, u32[]{:S(2)}) collective-permute-start(bf16[48,128]{1,0:T(8,128)(2,1)S(1)} %get-tuple-element.44), channel_id=1, source_target_pairs={{0,3},{1,2},{2,1},{3,0},{4,7},{5,6},{6,5},{7,4},{8,11},{9,10},{10,... | collective-permute-start | bytes 36872 | tf_op jit(solution)/shard_map/ppermute | solution.py:49
  19.4 1.0 %shard_map.137.main_ref = f32[32,1024]{1,0:T(8,128)S(1)} custom-call(f32[32,1024]{1,0:T(8,128)S(1)} %get-tuple-element.38.fw_ref, f32[2,32,1024]{2,1,0:T(8,128)S(1)} %get-tuple-element.33.stat_ref, bf16[80,128]{1,0:T(8,128)(2,1)S(1)} %collective-permute-done.3.a_ref.ha_ref, bf16[80,128]{1,0:T(8,128)(2,1)S(1)} %collective-permute-done.4.b_ref.hb_ref, ...), custom_call_target="tpu_custom_call" | custom-call | flops 400000000 | bytes 2000000 | tf_op jit(solution)/shard_map/pallas_call | solution.py:22
  20.4 0.5 %collective-permute-done.6.rb_ref = bf16[48,128]{1,0:T(8,128)(2,1)S(1)} collective-permute-done((bf16[48,128]{1,0:T(8,128)(2,1)S(1)}, bf16[48,128]{1,0:T(8,128)(2,1)S(1)}, u32[]{:S(2)}, u32[]{:S(2)}) %collective-permute-start.6) | collective-permute-done | bytes 12320 | tf_op jit(solution)/shard_map/ppermute | solution.py:49
  21.0 1.9 %shard_map.138 = (bf16[128,256]{1,0:T(8,128)(2,1)S(1)}, f32[16,128]{1,0:T(8,128)S(1)}, f32[16,128]{1,0:T(8,128)S(1)}, f32[16,128]{1,0:T(8,128)S(1)}, f32[16,128]{1,0:T(8,128)S(1)}) custom-call(f32[3,48,128]{2,1,0:T(8,128)S(1)} %get-tuple-element.43.strip_ref, bf16[48,128]{1,0:T(8,128)(2,1)S(1)} %collective-permute-done.5.ra_ref, ...), custom_call_target="tpu_custom_call" | custom-call | tf_op jit(solution)/shard_map/pallas_call | solution.py:22
  22.9 0.8 %collective-permute-start.7 = (f32[16,128]{1,0:T(8,128)S(1)}, f32[16,128]{1,0:T(8,128)S(1)}, u32[]{:S(2)}, u32[]{:S(2)}) collective-permute-start(f32[16,128]{1,0:T(8,128)S(1)} %get-tuple-element.57), channel_id=1, source_target_pairs={{0,8},{4,12},{8,0},{12,4},{1,9},{5,13},{9,1},{13,5},{2,10},{6,14},... | collective-permute-start | bytes 24584 | tf_op jit(solution)/shard_map/ppermute | solution.py:65
  23.7 2.0 %collective-permute-start.8 = (f32[16,128]{1,0:T(8,128)S(1)}, f32[16,128]{1,0:T(8,128)S(1)}, u32[]{:S(2)}, u32[]{:S(2)}) collective-permute-start(f32[16,128]{1,0:T(8,128)S(1)} %get-tuple-element.58), channel_id=1, source_target_pairs={{0,12},{4,8},{8,4},{12,0},{1,13},{5,9},{9,5},{13,1},{2,14},{6,10},... | collective-permute-start | bytes 24584 | tf_op jit(solution)/shard_map/ppermute | solution.py:65
  25.7 0.7 %collective-permute-start.9 = (f32[16,128]{1,0:T(8,128)S(1)}, f32[16,128]{1,0:T(8,128)S(1)}, u32[]{:S(2)}, u32[]{:S(2)}) collective-permute-start(f32[16,128]{1,0:T(8,128)S(1)} %get-tuple-element.59), channel_id=1, source_target_pairs={{0,4},{4,0},{8,12},{12,8},{1,5},{5,1},{9,13},{13,9},{2,6},{6,2},{1... | collective-permute-start | bytes 24584 | tf_op jit(solution)/shard_map/ppermute | solution.py:65
  26.4 0.6 %reshape.19 = bf16[32,4,256]{2,1,0:T(4,128)(2,1)} reshape(bf16[128,256]{1,0:T(8,128)(2,1)S(1)} %get-tuple-element.54) | data formatting | bytes 131072 | tf_op jit(solution)/shard_map/reshape | solution.py:600
  27.0 0.4 %collective-permute-done.7.rest_1_ = f32[16,128]{1,0:T(8,128)S(1)} collective-permute-done((f32[16,128]{1,0:T(8,128)S(1)}, f32[16,128]{1,0:T(8,128)S(1)}, u32[]{:S(2)}, u32[]{:S(2)}) %collective-permute-start.7) | collective-permute-done | bytes 8224 | tf_op jit(solution)/shard_map/ppermute | solution.py:65
  27.4 1.7 %collective-permute-done.8.rest_2_ = f32[16,128]{1,0:T(8,128)S(1)} collective-permute-done((f32[16,128]{1,0:T(8,128)S(1)}, f32[16,128]{1,0:T(8,128)S(1)}, u32[]{:S(2)}, u32[]{:S(2)}) %collective-permute-start.8) | collective-permute-done | bytes 8224 | tf_op jit(solution)/shard_map/ppermute | solution.py:65
  29.2 0.2 collective-permute-done.9.rest_3_
  29.4 0.8 %shard_map.139 = f32[256,128]{1,0:T(8,128)} custom-call(bf16[256,64]{1,0:T(8,128)(2,1)S(1)} %get-tuple-element.55.hot_ref, f32[16,128]{1,0:T(8,128)S(1)} %get-tuple-element.56.rest_0_, f32[16,128]{1,0:T(8,128)S(1)} %collective-permute-done.7.rest_1_, f32[16,128]{1,0:T(8,128)S(1)} %collective-permute-done.8.rest_2_, f32[16,128]{1,0:T(8,128)S(1)} %collective-permute-done.9.rest_3_), custom_call_target="tpu_custom_call" | custom-call | tf_op jit(solution)/shard_map/pallas_call | solution.py:22
  (6 shorter events, 0.0 us)
Async XLA Ops:
  1.7 7.6 %collective-permute-start = (bf16[16,128]{1,0:T(8,128)(2,1)S(1)}, bf16[16,128]{1,0:T(8,128)(2,1)S(1)}, u32[]{:S(2)}, u32[]{:S(2)}) collective-permute-start(bf16[16,128]{1,0:T(8,128)(2,1)S(1)} %get-tuple-element.35), channel_id=1, source_target_pairs={{0,8},{4,12},{8,0},{12,4},{1,9},{5,13},{9,1},{13,5},{2,10},{6,14},... | collective-permute-start | bytes 12296 | tf_op jit(solution)/shard_map/ppermute | solution.py:65
  5.8 5.4 %collective-permute-start.1 = (bf16[16,128]{1,0:T(8,128)(2,1)S(1)}, bf16[16,128]{1,0:T(8,128)(2,1)S(1)}, u32[]{:S(2)}, u32[]{:S(2)}) collective-permute-start(bf16[16,128]{1,0:T(8,128)(2,1)S(1)} %get-tuple-element.36), channel_id=1, source_target_pairs={{0,12},{4,8},{8,4},{12,0},{1,13},{5,9},{9,5},{13,1},{2,14},{6,10},... | collective-permute-start | bytes 12296 | tf_op jit(solution)/shard_map/ppermute | solution.py:65
  7.1 4.1 %collective-permute-start.2 = (bf16[16,128]{1,0:T(8,128)(2,1)S(1)}, bf16[16,128]{1,0:T(8,128)(2,1)S(1)}, u32[]{:S(2)}, u32[]{:S(2)}) collective-permute-start(bf16[16,128]{1,0:T(8,128)(2,1)S(1)} %get-tuple-element.37), channel_id=1, source_target_pairs={{0,4},{4,0},{8,12},{12,8},{1,5},{5,1},{9,13},{13,9},{2,6},{6,2},{1... | collective-permute-start | bytes 12296 | tf_op jit(solution)/shard_map/ppermute | solution.py:65
  11.7 5.8 %collective-permute-start.3 = (bf16[80,128]{1,0:T(8,128)(2,1)S(1)}, bf16[80,128]{1,0:T(8,128)(2,1)S(1)}, u32[]{:S(2)}, u32[]{:S(2)}) collective-permute-start(bf16[80,128]{1,0:T(8,128)(2,1)S(1)} %get-tuple-element.41), channel_id=1, source_target_pairs={{0,4},{4,0},{8,12},{12,8},{1,5},{5,1},{9,13},{13,9},{2,6},{6,2},{1... | collective-permute-start | bytes 61448 | tf_op jit(solution)/shard_map/ppermute | solution.py:49
  11.8 5.7 %collective-permute-start.4 = (bf16[80,128]{1,0:T(8,128)(2,1)S(1)}, bf16[80,128]{1,0:T(8,128)(2,1)S(1)}, u32[]{:S(2)}, u32[]{:S(2)}) collective-permute-start(bf16[80,128]{1,0:T(8,128)(2,1)S(1)} %get-tuple-element.42), channel_id=1, source_target_pairs={{0,12},{4,8},{8,4},{12,0},{1,13},{5,9},{9,5},{13,1},{2,14},{6,10},... | collective-permute-start | bytes 61448 | tf_op jit(solution)/shard_map/ppermute | solution.py:49
  17.8 2.7 %collective-permute-start.5 = (bf16[48,128]{1,0:T(8,128)(2,1)S(1)}, bf16[48,128]{1,0:T(8,128)(2,1)S(1)}, u32[]{:S(2)}, u32[]{:S(2)}) collective-permute-start(bf16[48,128]{1,0:T(8,128)(2,1)S(1)} %get-tuple-element.44), channel_id=1, source_target_pairs={{0,1},{1,0},{2,3},{3,2},{4,5},{5,4},{6,7},{7,6},{8,9},{9,8},{10,11... | collective-permute-start | bytes 36872 | tf_op jit(solution)/shard_map/ppermute | solution.py:49
  17.8 3.2 %collective-permute-start.6 = (bf16[48,128]{1,0:T(8,128)(2,1)S(1)}, bf16[48,128]{1,0:T(8,128)(2,1)S(1)}, u32[]{:S(2)}, u32[]{:S(2)}) collective-permute-start(bf16[48,128]{1,0:T(8,128)(2,1)S(1)} %get-tuple-element.44), channel_id=1, source_target_pairs={{0,3},{1,2},{2,1},{3,0},{4,7},{5,6},{6,5},{7,4},{8,11},{9,10},{10,... | collective-permute-start | bytes 36872 | tf_op jit(solution)/shard_map/ppermute | solution.py:49
  22.9 4.6 %collective-permute-start.7 = (f32[16,128]{1,0:T(8,128)S(1)}, f32[16,128]{1,0:T(8,128)S(1)}, u32[]{:S(2)}, u32[]{:S(2)}) collective-permute-start(f32[16,128]{1,0:T(8,128)S(1)} %get-tuple-element.57), channel_id=1, source_target_pairs={{0,8},{4,12},{8,0},{12,4},{1,9},{5,13},{9,1},{13,5},{2,10},{6,14},... | collective-permute-start | bytes 24584 | tf_op jit(solution)/shard_map/ppermute | solution.py:65
  23.7 5.5 %collective-permute-start.8 = (f32[16,128]{1,0:T(8,128)S(1)}, f32[16,128]{1,0:T(8,128)S(1)}, u32[]{:S(2)}, u32[]{:S(2)}) collective-permute-start(f32[16,128]{1,0:T(8,128)S(1)} %get-tuple-element.58), channel_id=1, source_target_pairs={{0,12},{4,8},{8,4},{12,0},{1,13},{5,9},{9,5},{13,1},{2,14},{6,10},... | collective-permute-start | bytes 24584 | tf_op jit(solution)/shard_map/ppermute | solution.py:65
  25.7 3.7 %collective-permute-start.9 = (f32[16,128]{1,0:T(8,128)S(1)}, f32[16,128]{1,0:T(8,128)S(1)}, u32[]{:S(2)}, u32[]{:S(2)}) collective-permute-start(f32[16,128]{1,0:T(8,128)S(1)} %get-tuple-element.59), channel_id=1, source_target_pairs={{0,4},{4,0},{8,12},{12,8},{1,5},{5,1},{9,13},{13,9},{2,6},{6,2},{1... | collective-permute-start | bytes 24584 | tf_op jit(solution)/shard_map/ppermute | solution.py:65

commit v4 on v3

--- a/solution.py
+++ b/solution.py
@@ -193,40 +193,54 @@
     copies[-1].wait()
 
 
-def forward_kernel(n, rows, axial_ref, foot_ref, stat_ref, *rest):
-    pieces, (fw_ref, a_ref, b_ref, slots_s, flat, edge) = rest[:-6], rest[-6:]
-    me = lax.axis_index("view")
+def project(lhs, foot_ref, start, rows):
+    owner = iota((16, foot_ref.shape[2]), 0) // rows
+    got = None
+    for i in range(16 // rows):
+        one = jnp.dot(lhs, foot_ref[start + i], preferred_element_type=F32)
+        got = one if got is None else jnp.where(owner == i, one, got)
+    return got.astype(BF16).astype(F32)
+
+
+def edge_kernel(n, rows, axial_ref, foot_ref, stat_ref, *rest):
+    pieces, (slots_ref, a_ref, b_ref, flat, edge) = rest[:-5], rest[-5:]
     views = foot_ref.shape[0]
     if len(pieces) > 1:
         cap = pieces[0].shape[0]
         for k in range(n):
-            slots_s[pl.ds(pl.multiple_of(partner(n, True, k) * cap, cap), cap), :] = pieces[k][...]
-        slot_rows = slots_s[...]
+            slots_ref[pl.ds(pl.multiple_of(partner(n, True, k) * cap, cap), cap), :] = pieces[k][...]
     else:
-        slot_rows = pieces[0][...]
-    axial_sum = jnp.dot(axial_ref[...], slot_rows, preferred_element_type=F32).astype(BF16)
-    per = 16 // rows
-    owner = lax.broadcasted_iota(jnp.int32, (16, foot_ref.shape[2]), 0) // rows
-    for q in range(views // per):
-        lhs = axial_sum[16 * q : 16 * q + 16, :]
-        got = None
-        for i in range(per):
-            one = jnp.dot(lhs, foot_ref[q * per + i], preferred_element_type=F32)
-            got = one if got is None else jnp.where(owner == i, one, got)
-        put_flat(flat, 16 * q, got.astype(BF16).astype(F32))
-    fw = widen(flat, rows)
-    fw_ref[...] = fw
+        slots_ref[...] = pieces[0][...]
+    per, both = 16 // rows, views * rows
+    ends = jnp.concatenate([axial_ref[0:16, :], axial_ref[both - 16 : both, :]], axis=0)
+    axial_sum = jnp.dot(ends, slots_ref[...], preferred_element_type=F32).astype(BF16)
+    for way, start in ((0, 0), (1, views - per)):
+        put_flat(flat, 16 * way, project(axial_sum[16 * way : 16 * way + 16, :], foot_ref, start, rows))
     edge[...] = jnp.zeros(edge.shape, F32)
+    tiles = flat.shape[0]
     for way, start in ((0, 0), (1, views - HALO)):
-        for c in range(3):
-            part = fw[start : start + HALO, :] if c == 1 else stat_ref[c // 2, start : start + HALO, :]
-            for t in range(part.shape[1] // LANES):
-                at = (3 * t + c) * HALO
-                edge[way, at : at + HALO, :] = part[:, t * LANES : (t + 1) * LANES]
-    even = me % 2 == 0
+        first = 16 * way + (start - way * (views - per)) * rows
+        for r in range(rows):
+            for t in range(tiles):
+                at = 3 * (r * tiles + t) * HALO
+                lanes = slice((r * tiles + t) * LANES, (r * tiles + t + 1) * LANES)
+                edge[way, at : at + HALO, :] = stat_ref[0, start : start + HALO, lanes]
+                edge[way, at + HALO : at + 2 * HALO, :] = flat[t, pl.ds(first + r, HALO, stride=rows), :]
+                edge[way, at + 2 * HALO : at + 3 * HALO, :] = stat_ref[1, start : start + HALO, lanes]
+    even = lax.axis_index("view") % 2 == 0
     to_prev, to_next = edge[0], edge[1]
     a_ref[...] = jnp.where(even, to_next, to_prev).astype(BF16)
     b_ref[...] = jnp.where(even, to_prev, to_next).astype(BF16)
+
+
+def forward_kernel(rows, axial_ref, foot_ref, slots_ref, ends_ref, fw_ref, flat):
+    axial_sum = jnp.dot(axial_ref[...], slots_ref[...], preferred_element_type=F32).astype(BF16)
+    per, both = 16 // rows, flat.shape[1]
+    for q in range(1, both // 16 - 1):
+        put_flat(flat, 16 * q, project(axial_sum[16 * q : 16 * q + 16, :], foot_ref, q * per, rows))
+    flat[:, 0:16, :] = ends_ref[:, 0:16, :]
+    flat[:, both - 16 : both, :] = ends_ref[:, 16:32, :]
+    fw_ref[...] = widen(flat, rows)
 
 
 def sort_halo(a_ref, b_ref, halo):
@@ -241,13 +255,11 @@
     return jnp.concatenate([halo[way, at : at + HALO, :] for at in starts], axis=1)
 
 
-def strip_of(wide, rows, inner):
-    cols = wide.shape[1] // rows
-    at = iota((wide.shape[0], LANES), 1)
-    total = jnp.zeros((wide.shape[0], LANES), F32)
+def strip_of(tile, rows, tiles, inner):
+    total = None
     for r in range(rows):
-        head = wide[:, r * cols : r * cols + LANES]
-        tail = wide[:, (r + 1) * cols - LANES : (r + 1) * cols]
+        head, tail = tile(r * tiles), tile((r + 1) * tiles - 1)
+        at = iota(head.shape, 1)
         left, right = 16 * r, 64 + 16 * r
         if inner:
             picks = ((head, 0, left + HALO, 6), (tail, LANES - 6, right, 6))
@@ -255,31 +267,39 @@
             picks = ((tail, LANES - HALO, left, HALO), (head, 0, right + 6, HALO))
         for source, begin, target, width in picks:
             moved = pltpu.roll(source, (target - begin) % LANES, 1)
-            total = jnp.where((at >= target) & (at < target + width), moved, total)
+            rest = jnp.zeros_like(moved) if total is None else total
+            total = jnp.where((at >= target) & (at < target + width), moved, rest)
     return total
 
 
-def own_strip_kernel(rows, fw_ref, stat_ref, in_ref, msg_ref):
-    for c in range(3):
-        wide = fw_ref[...] if c == 1 else stat_ref[c // 2]
-        in_ref[c] = strip_of(wide, rows, True)
-        msg_ref[c] = strip_of(wide, rows, False)
-
-
-def strip_message_kernel(rows, wide, in_ref, msg_ref, a_ref, b_ref, strip_ref, out_ref, buf, halo):
-    views = in_ref.shape[1]
+def joined(parts):
+    return parts[0] + pltpu.roll(parts[1], HALO, 1) + pltpu.roll(parts[2], 2 * HALO, 1)
+
+
+def own_strips(rows, fw_ref, stat_ref, inner):
+    tiles = fw_ref.shape[1] // rows // LANES
+    sources = (stat_ref.at[0], fw_ref, stat_ref.at[1])
+    get = [lambda i, ref=ref: ref[:, i * LANES : (i + 1) * LANES] for ref in sources]
+    return [strip_of(tile, rows, tiles, inner) for tile in get]
+
+
+def own_message_kernel(rows, fw_ref, stat_ref, msg_ref):
+    msg_ref[...] = joined(own_strips(rows, fw_ref, stat_ref, False))
+
+
+def halo_strip(halo, way, rows, tiles, inner):
+    return strip_of(lambda i: halo[way, 3 * i * HALO : 3 * (i + 1) * HALO, :], rows, tiles, inner)
+
+
+def strip_message_kernel(rows, tiles, msg_ref, a_ref, b_ref, out_ref, buf, halo):
+    views = msg_ref.shape[0]
     sort_halo(a_ref, b_ref, halo)
-    buf[...] = jnp.zeros(buf.shape, F32)
-    strip_ref[...] = jnp.zeros(strip_ref.shape, F32)
-    for c in range(3):
-        for way, start in ((0, 0), (1, HALO + views)):
-            part = halo_of(halo, way, c, wide)
-            strip_ref[c, start : start + HALO, :] = strip_of(part, rows, True)
-            buf[c, start : start + HALO, :] = strip_of(part, rows, False)
-        strip_ref[c, HALO : HALO + views, :] = in_ref[c]
-        buf[c, HALO : HALO + views, :] = msg_ref[c]
-    total = buf[0] + pltpu.roll(buf[1], HALO, 1) + pltpu.roll(buf[2], 2 * HALO, 1)
-    out_ref[...] = total.astype(BF16)
+    buf[HALO + views :, :] = jnp.zeros((buf.shape[0] - HALO - views, LANES), F32)
+    buf[HALO : HALO + views, :] = msg_ref[...]
+    for way, start in ((0, 0), (1, HALO + views)):
+        part = halo_strip(halo, way, rows, tiles, False)
+        buf[start : start + HALO, :] = joined([part[c * HALO : (c + 1) * HALO, :] for c in range(3)])
+    out_ref[...] = buf[...].astype(BF16)
 
 
 def prelu(z, slopes_ref):
@@ -349,29 +369,32 @@
             update[STEP * k : STEP * k + part, at] = out[0:part, :]
 
 
-def inner_kernel(fw_ref, stat_ref, w1, w2, w3, a1, a2, out_ref, one_ref, two_ref, x, s1, s2, s3, update):
+def inner_kernel(fw_ref, stat_ref, w1, w2, a1, a2, one_ref, s3, x, s1, s2):
     views = fw_ref.shape[0]
-    channels = a1.shape[0]
     x[...] = jnp.zeros(x.shape, F32)
     for c in range(3):
         x[c, 0:views, :] = fw_ref[...] if c == 1 else stat_ref[c // 2]
     first_layer(lambda c, at: x[c, :, at], views - 2, w1, a1, s1, s2)
     second_layer(views - 4, w2, a2, s2, s3)
-    last_layer(views - 6, channels, w3, s3, update)
-    out_ref[HALO : views - HALO, :] = stat_ref[0, HALO : views - HALO, :] + update[...]
-    two = 2 * channels
-    for ref, ends in ((one_ref, s2.at[1]), (two_ref, s3)):
-        end = ends.shape[0]
-        ref[0:two, :] = ends[0:two, :]
-        ref[two : 2 * two, :] = ends[end - two : end, :]
+    two, end = 2 * a1.shape[0], s2.shape[1]
+    one_ref[0:two, :] = s2[1, 0:two, :]
+    one_ref[two : 2 * two, :] = s2[1, end - two : end, :]
 
 
 def outer_kernel(
-    fw_ref, stat_ref, ha_ref, hb_ref, in_ref, one_ref, two_ref, w1, w2, w3, a1, a2, out_ref, x, halo, s1, s2, s3, update
+    rows, fw_ref, stat_ref, ha_ref, hb_ref, one_ref, two_ref, w1, w2, w3, a1, a2, out_ref, strip_ref, x, halo, s1, s2, s3,
+    update, inner
 ):
     views, wide = fw_ref.shape
     channels = a1.shape[0]
     sort_halo(ha_ref, hb_ref, halo)
+    strip_ref[...] = jnp.zeros(strip_ref.shape, F32)
+    for way, start in ((0, 0), (1, HALO + views)):
+        part = halo_strip(halo, way, rows, wide // rows // LANES, True)
+        for c in range(3):
+            strip_ref[c, start : start + HALO, :] = part[c * HALO : (c + 1) * HALO, :]
+    for c, own in enumerate(own_strips(rows, fw_ref, stat_ref, True)):
+        strip_ref[c, HALO : HALO + views, :] = own
     x[...] = jnp.zeros(x.shape, F32)
     for c in range(3):
         x[0, c, 0:HALO, :] = halo_of(halo, 0, c, wide)
@@ -386,14 +409,16 @@
         for at in chunks(one_ref):
             for b, moved in enumerate(shifted(one_ref[kept, at])):
                 s2[side, b, old[side] : old[side] + two, at] = moved
-        s3[side, old[side] : old[side] + two, :] = two_ref[kept, :]
+        end = side * (two_ref.shape[0] - two)
+        s3[side, old[side] : old[side] + two, :] = two_ref[end : end + two, :]
     for side in range(2):
         first_layer(lambda c, at: x[side, c, :, at], HALO, w1, a1, s1.at[side], s2.at[side], new[side])
     for side in range(2):
         second_layer(HALO, w2, a2, s2.at[side], s3.at[side], new[side])
     for side in range(2):
         last_layer(HALO, channels, w3, s3.at[side], update.at[side])
-    out_ref[HALO : views - HALO, :] = in_ref[HALO : views - HALO, :]
+    last_layer(views - 2 * HALO, channels, w3, two_ref, inner)
+    out_ref[HALO : views - HALO, :] = stat_ref[0, HALO : views - HALO, :] + inner[...]
     for side, begin in ((0, 0), (1, views - HALO)):
         out_ref[begin : begin + HALO, :] = stat_ref[0, begin : begin + HALO, :] + update[side]
 
@@ -537,23 +562,33 @@
     message_rows = -(-9 * (wide // LANES) // 16) * 16
     edge = shape((message_rows, LANES), BF16)
     halo = pltpu.VMEM((2, message_rows, LANES), F32)
-    fw, edge_a, edge_b = call(
-        functools.partial(forward_kernel, n, rows),
-        [shape((views, wide)), edge, edge],
-        [pltpu.VMEM((n * slots, vox), BF16), flat, halo],
+    slot_rows, edge_a, edge_b, ends = call(
+        functools.partial(edge_kernel, n, rows),
+        [shape((n * slots, vox), BF16), edge, edge, shape((cols // LANES, 32, LANES))],
+        [halo],
         [axial_flat, foot, stat, *incoming],
     )
     halo_a, halo_b = both_ways(edge_a, edge_b, "view")
-    own = shape((3, views, LANES))
-    strip_in, strip_msg = call(
-        functools.partial(own_strip_kernel, rows), [own, own], [], [fw, stat], cost=(10**7, 10**6)
+    fw = call(
+        functools.partial(forward_kernel, rows),
+        shape((views, wide)),
+        [flat],
+        [axial_flat, foot, slot_rows, ends],
+        cost=(10**6, 10**4),
+    )
+    strip_msg = call(
+        functools.partial(own_message_kernel, rows),
+        shape((views, LANES)),
+        [],
+        [fw, stat],
+        cost=(10**6, 10**4),
     )
     padded = 48
-    strip, message = call(
-        functools.partial(strip_message_kernel, rows, wide),
-        [shape((3, padded, LANES)), shape((padded, LANES), BF16)],
-        [pltpu.VMEM((3, padded, LANES), F32), halo],
-        [strip_in, strip_msg, halo_a, halo_b],
+    message = call(
+        functools.partial(strip_message_kernel, rows, cols // LANES),
+        shape((padded, LANES), BF16),
+        [pltpu.VMEM((padded, LANES), F32), halo],
+        [strip_msg, halo_a, halo_b],
     )
     side_a, side_b = both_ways(message, message, "col")
 
@@ -567,19 +602,24 @@
         ]
 
     weights = [w1, w2, w3, a1, a2]
-    ends = shape((4 * channels, wide), BF16)
-    inner, one, two = call(
+    count = views - 2 * HALO
+    one, two = call(
         inner_kernel,
-        [shape((views, wide)), ends, ends],
-        [pltpu.VMEM((3, views + BAND, wide), F32), *net_scratch(views - 2 * HALO, wide)],
-        [fw, stat, *weights],
-        cost=(2 * 10**9, 4 * 10**6),
-    )
-    main = call(
-        outer_kernel,
-        shape((views, wide)),
-        [pltpu.VMEM((2, 3, 2 * BAND, wide), F32), halo, *net_scratch(HALO, wide, HALO, 2)],
-        [fw, stat, halo_a, halo_b, inner, one, two, *weights],
+        [shape((4 * channels, wide), BF16), shape(((count + 2) * channels, wide), BF16)],
+        [pltpu.VMEM((3, views + BAND, wide), F32), *net_scratch(count, wide)[:2]],
+        [fw, stat, w1, w2, a1, a2],
+        cost=(10**6, 10**4),
+    )
+    main, strip = call(
+        functools.partial(outer_kernel, rows),
+        [shape((views, wide)), shape((3, padded, LANES))],
+        [
+            pltpu.VMEM((2, 3, 2 * BAND, wide), F32),
+            halo,
+            *net_scratch(HALO, wide, HALO, 2),
+            pltpu.VMEM((count, wide), F32),
+        ],
+        [fw, stat, halo_a, halo_b, one, two, *weights],
         cost=(4 * 10**8, 2 * 10**6),
     )
     parts = [shape((slots, vox))] * n if split else [shape((n * slots, vox))]

time: 30.4 us -> 30.1 us (level)
  waiting for transfers between devices: 4.73 us -> 4.31 us
    ppermute x2, waiting for transfers between devices: 0.55 us -> 0.13 us  [both_ways(): lax.ppermute(array_b, axis, second)]
    pallas_call x9 -> x10, Pallas kernels: 10.5 us -> 10.7 us  [call(): pl.pallas_call(body, out_shape=outs if single else list(outs), in_specs=s...]
  transfers between devices with their start and end apart: 10 -> 10, of which waited for: 5 -> 5; matrix products, arithmetic and copies ran while one was open for 2% -> 2% of each run, Pallas kernels for 20% -> 21%
where the time goes in v4:
time: 30.1 us; the launch traced here: 29.9 us
  starting transfers between devices  13.5 us (45%)
  Pallas kernels  10.7 us (36%)
  waiting for transfers between devices  4.31 us (14%)
  between operations  0.72 us (2%)
  local copies, waits for them, and re-layouts  0.65 us (2%)
    pallas_call x10, Pallas kernels, call(): pl.pallas_call(body, out_shape=outs if single else list(outs), in_specs=s...  10.7 us
    ppermute x6, starting transfers between devices, exchange(): lax.ppermute(p, axis, [(i, i ^ k) for i in range(n)])  9.19 us
    ppermute x2, starting transfers between devices, both_ways(): lax.ppermute(array_b, axis, second)  4.28 us
    ppermute x6, waiting for transfers between devices, exchange(): lax.ppermute(p, axis, [(i, i ^ k) for i in range(n)])  4.18 us
    reshape x1, local copies, waits for them, and re-layouts, shards(): return (dual_out.reshape(views, rows, cols), backprojection)  0.65 us
  transfers between devices with their start and end apart: 10, of which 5 were waited for; matrix products, arithmetic and copies ran while one was open for 2% of the time, Pallas kernels for 21%

profile of v4, /device:TPU:0, one launch (start us, length us, event | category | flops | bytes accessed | tf_op | source)
XLA Modules:
  0.0 29.9 jit_solution(2630804409664073119)
XLA Ops:
  0.6 1.0 %shard_map.132 = (bf16[16,128]{1,0:T(8,128)(2,1)S(1)}, bf16[16,128]{1,0:T(8,128)(2,1)S(1)}, bf16[16,128]{1,0:T(8,128)(2,1)S(1)}, bf16[16,128]{1,0:T(8,128)(2,1)S(1)}) custom-call(s32[1,4,16]{2,1,0:T(4,128)} %req_hbm.1, s32[1,4]{1,0:T(1,128)} %cnt_hbm.1, bf16[256,128]{1,0:T(8,128)(2,1)} %vol_hbm.1), custom_call_target="tpu_custom_call" | custom-call | tf_op jit(solution)/shard_map/pallas_call | solution.py:22
  1.7 4.1 %collective-permute-start = (bf16[16,128]{1,0:T(8,128)(2,1)S(1)}, bf16[16,128]{1,0:T(8,128)(2,1)S(1)}, u32[]{:S(2)}, u32[]{:S(2)}) collective-permute-start(bf16[16,128]{1,0:T(8,128)(2,1)S(1)} %get-tuple-element.33), channel_id=1, source_target_pairs={{0,8},{4,12},{8,0},{12,4},{1,9},{5,13},{9,1},{13,5},{2,10},{6,14},... | collective-permute-start | bytes 12296 | tf_op jit(solution)/shard_map/ppermute | solution.py:65
  5.8 1.3 %collective-permute-start.1 = (bf16[16,128]{1,0:T(8,128)(2,1)S(1)}, bf16[16,128]{1,0:T(8,128)(2,1)S(1)}, u32[]{:S(2)}, u32[]{:S(2)}) collective-permute-start(bf16[16,128]{1,0:T(8,128)(2,1)S(1)} %get-tuple-element.34), channel_id=1, source_target_pairs={{0,12},{4,8},{8,4},{12,0},{1,13},{5,9},{9,5},{13,1},{2,14},{6,10},... | collective-permute-start | bytes 12296 | tf_op jit(solution)/shard_map/ppermute | solution.py:65
  7.1 0.2 collective-permute-start.2
  7.4 2.0 %shard_map.131 = (f32[2,32,1024]{2,1,0:T(8,128)S(1)}, bf16[32,128,256]{2,1,0:T(8,128)(2,1)S(1)}, bf16[128,64]{1,0:T(8,128)(2,1)S(1)}, bf16[64,128]{1,0:T(8,128)(...) custom-call(bf16[32,4,256]{2,1,0:T(4,128)(2,1)} %refs_0_.1, ...), custom_call_target="tpu_custom_call" | custom-call | flops 100000000 | bytes 4000000 | tf_op jit(solution)/shard_map/pallas_call | solution.py:22
  9.3 1.9 %collective-permute-done.1.rest_2_ = bf16[16,128]{1,0:T(8,128)(2,1)S(1)} collective-permute-done((bf16[16,128]{1,0:T(8,128)(2,1)S(1)}, bf16[16,128]{1,0:T(8,128)(2,1)S(1)}, u32[]{:S(2)}, u32[]{:S(2)}) %collective-permute-start.1) | collective-permute-done | bytes 4128 | tf_op jit(solution)/shard_map/ppermute | solution.py:65
  11.2 0.3 %shard_map.133 = (bf16[64,128]{1,0:T(8,128)(2,1)S(1)}, bf16[80,128]{1,0:T(8,128)(2,1)S(1)}, bf16[80,128]{1,0:T(8,128)(2,1)S(1)}, f32[2,32,128]{2,1,0:T(8,128)S(1)}) custom-call(bf16[128,64]{1,0:T(8,128)(2,1)S(1)} %get-tuple-element.29.axial_ref, bf16[32,128,256]{2,1,0:T(8,128)(2,1)S(1)} %get-tuple-element.30.foot_ref, ...), custom_call_target="tpu_custom_call" | custom-call | tf_op jit(solution)/shard_map/pallas_call | solution.py:22
  11.6 2.7 %collective-permute-start.4 = (bf16[80,128]{1,0:T(8,128)(2,1)S(1)}, bf16[80,128]{1,0:T(8,128)(2,1)S(1)}, u32[]{:S(2)}, u32[]{:S(2)}) collective-permute-start(bf16[80,128]{1,0:T(8,128)(2,1)S(1)} %get-tuple-element.39), channel_id=1, source_target_pairs={{0,12},{4,8},{8,4},{12,0},{1,13},{5,9},{9,5},{13,1},{2,14},{6,10},... | collective-permute-start | bytes 61448 | tf_op jit(solution)/shard_map/ppermute | solution.py:49
  14.3 0.4 %shard_map.134.fw_ref = f32[32,1024]{1,0:T(8,128)S(1)} custom-call(bf16[128,64]{1,0:T(8,128)(2,1)S(1)} %get-tuple-element.29.axial_ref, bf16[32,128,256]{2,1,0:T(8,128)(2,1)S(1)} %get-tuple-element.30.foot_ref, bf16[64,128]{1,0:T(8,128)(2,1)S(1)} %get-tuple-element.36.slots_ref, f32[2,32,128]{2,1,0:T(8,128)S(1)} %get-tuple-element.37.ends_ref), custom_call_target="tpu_custom_call" | custom-call | flops 1000000 | bytes 10000 | tf_op jit(solution)/shard_map/pallas_call | solution.py:22
  14.7 0.3 shard_map.137.msg_ref
  15.0 2.3 %shard_map.135 = (bf16[128,1024]{1,0:T(8,128)(2,1)S(1)}, bf16[896,1024]{1,0:T(8,128)(2,1)S(1)}) custom-call(f32[32,1024]{1,0:T(8,128)S(1)} %shard_map.134.fw_ref, f32[2,32,1024]{2,1,0:T(8,128)S(1)} %get-tuple-element.31.stat_ref, bf16[256,144]{1,0:T(8,128)(2,1)S(1)} %get-tuple-element.40.w1, bf16[192,768]{1,0:T(8,128)(2,1)S(1)} %get-tuple-element.41.w2, ...), custom_call_target="tpu_custom_call" | custom-call | flops 1000000 | bytes 10000 | tf_op jit(solution)/shard_map/pallas_call | solution.py:22
  17.3 0.2 shard_map.138
  17.5 1.6 %collective-permute-start.6 = (bf16[48,128]{1,0:T(8,128)(2,1)S(1)}, bf16[48,128]{1,0:T(8,128)(2,1)S(1)}, u32[]{:S(2)}, u32[]{:S(2)}) collective-permute-start(bf16[48,128]{1,0:T(8,128)(2,1)S(1)} %shard_map.138), channel_id=1, source_target_pairs={{0,3},{1,2},{2,1},{3,0},{4,7},{5,6},{6,5},{7,4},{8,11},{9,10},{10,... | collective-permute-start | bytes 36872 | tf_op jit(solution)/shard_map/ppermute | solution.py:49
  19.1 1.4 %shard_map.136 = (f32[32,1024]{1,0:T(8,128)S(1)}, f32[3,48,128]{2,1,0:T(8,128)S(1)}) custom-call(f32[32,1024]{1,0:T(8,128)S(1)} %shard_map.134.fw_ref, f32[2,32,1024]{2,1,0:T(8,128)S(1)} %get-tuple-element.31.stat_ref, bf16[80,128]{1,0:T(8,128)(2,1)S(1)} %collective-permute-done.3.ha_ref.a_ref, bf16[80,128]{1,0:T(8,128)(2,1)S(1)} %collective-permute-done.4.hb_ref.b_ref, ...), custom_call_target="tpu_custom_call" | custom-call | flops 400000000 | bytes 2000000 | tf_op jit(solution)/shard_map/pallas_call | solution.py:22
  20.6 0.1 collective-permute-done.6.rb_ref
  20.7 1.9 %shard_map.139 = (bf16[128,256]{1,0:T(8,128)(2,1)S(1)}, f32[16,128]{1,0:T(8,128)S(1)}, f32[16,128]{1,0:T(8,128)S(1)}, f32[16,128]{1,0:T(8,128)S(1)}, f32[16,128]{1,0:T(8,128)S(1)}) custom-call(f32[3,48,128]{2,1,0:T(8,128)S(1)} %get-tuple-element.47.strip_ref, bf16[48,128]{1,0:T(8,128)(2,1)S(1)} %collective-permute-done.5.ra_ref, ...), custom_call_target="tpu_custom_call" | custom-call | tf_op jit(solution)/shard_map/pallas_call | solution.py:22
  22.6 0.8 %collective-permute-start.7 = (f32[16,128]{1,0:T(8,128)S(1)}, f32[16,128]{1,0:T(8,128)S(1)}, u32[]{:S(2)}, u32[]{:S(2)}) collective-permute-start(f32[16,128]{1,0:T(8,128)S(1)} %get-tuple-element.53), channel_id=1, source_target_pairs={{0,8},{4,12},{8,0},{12,4},{1,9},{5,13},{9,1},{13,5},{2,10},{6,14},... | collective-permute-start | bytes 24584 | tf_op jit(solution)/shard_map/ppermute | solution.py:65
  23.4 2.0 %collective-permute-start.8 = (f32[16,128]{1,0:T(8,128)S(1)}, f32[16,128]{1,0:T(8,128)S(1)}, u32[]{:S(2)}, u32[]{:S(2)}) collective-permute-start(f32[16,128]{1,0:T(8,128)S(1)} %get-tuple-element.54), channel_id=1, source_target_pairs={{0,12},{4,8},{8,4},{12,0},{1,13},{5,9},{9,5},{13,1},{2,14},{6,10},... | collective-permute-start | bytes 24584 | tf_op jit(solution)/shard_map/ppermute | solution.py:65
  25.4 0.7 %collective-permute-start.9 = (f32[16,128]{1,0:T(8,128)S(1)}, f32[16,128]{1,0:T(8,128)S(1)}, u32[]{:S(2)}, u32[]{:S(2)}) collective-permute-start(f32[16,128]{1,0:T(8,128)S(1)} %get-tuple-element.55), channel_id=1, source_target_pairs={{0,4},{4,0},{8,12},{12,8},{1,5},{5,1},{9,13},{13,9},{2,6},{6,2},{1... | collective-permute-start | bytes 24584 | tf_op jit(solution)/shard_map/ppermute | solution.py:65
  26.1 0.6 %reshape.19 = bf16[32,4,256]{2,1,0:T(4,128)(2,1)} reshape(bf16[128,256]{1,0:T(8,128)(2,1)S(1)} %get-tuple-element.50) | data formatting | bytes 131072 | tf_op jit(solution)/shard_map/reshape | solution.py:640
  26.8 0.4 %collective-permute-done.7.rest_1_ = f32[16,128]{1,0:T(8,128)S(1)} collective-permute-done((f32[16,128]{1,0:T(8,128)S(1)}, f32[16,128]{1,0:T(8,128)S(1)}, u32[]{:S(2)}, u32[]{:S(2)}) %collective-permute-start.7) | collective-permute-done | bytes 8224 | tf_op jit(solution)/shard_map/ppermute | solution.py:65
  27.2 1.7 %collective-permute-done.8.rest_2_ = f32[16,128]{1,0:T(8,128)S(1)} collective-permute-done((f32[16,128]{1,0:T(8,128)S(1)}, f32[16,128]{1,0:T(8,128)S(1)}, u32[]{:S(2)}, u32[]{:S(2)}) %collective-permute-start.8) | collective-permute-done | bytes 8224 | tf_op jit(solution)/shard_map/ppermute | solution.py:65
  28.9 0.2 collective-permute-done.9.rest_3_
  29.1 0.8 %shard_map.140 = f32[256,128]{1,0:T(8,128)} custom-call(bf16[256,64]{1,0:T(8,128)(2,1)S(1)} %get-tuple-element.51.hot_ref, f32[16,128]{1,0:T(8,128)S(1)} %get-tuple-element.52.rest_0_, f32[16,128]{1,0:T(8,128)S(1)} %collective-permute-done.7.rest_1_, f32[16,128]{1,0:T(8,128)S(1)} %collective-permute-done.8.rest_2_, f32[16,128]{1,0:T(8,128)S(1)} %collective-permute-done.9.rest_3_), custom_call_target="tpu_custom_call" | custom-call | tf_op jit(solution)/shard_map/pallas_call | solution.py:22
  (7 shorter events, 0.1 us)
Async XLA Ops:
  1.7 7.6 %collective-permute-start = (bf16[16,128]{1,0:T(8,128)(2,1)S(1)}, bf16[16,128]{1,0:T(8,128)(2,1)S(1)}, u32[]{:S(2)}, u32[]{:S(2)}) collective-permute-start(bf16[16,128]{1,0:T(8,128)(2,1)S(1)} %get-tuple-element.33), channel_id=1, source_target_pairs={{0,8},{4,12},{8,0},{12,4},{1,9},{5,13},{9,1},{13,5},{2,10},{6,14},... | collective-permute-start | bytes 12296 | tf_op jit(solution)/shard_map/ppermute | solution.py:65
  5.8 5.4 %collective-permute-start.1 = (bf16[16,128]{1,0:T(8,128)(2,1)S(1)}, bf16[16,128]{1,0:T(8,128)(2,1)S(1)}, u32[]{:S(2)}, u32[]{:S(2)}) collective-permute-start(bf16[16,128]{1,0:T(8,128)(2,1)S(1)} %get-tuple-element.34), channel_id=1, source_target_pairs={{0,12},{4,8},{8,4},{12,0},{1,13},{5,9},{9,5},{13,1},{2,14},{6,10},... | collective-permute-start | bytes 12296 | tf_op jit(solution)/shard_map/ppermute | solution.py:65
  7.1 4.1 %collective-permute-start.2 = (bf16[16,128]{1,0:T(8,128)(2,1)S(1)}, bf16[16,128]{1,0:T(8,128)(2,1)S(1)}, u32[]{:S(2)}, u32[]{:S(2)}) collective-permute-start(bf16[16,128]{1,0:T(8,128)(2,1)S(1)} %get-tuple-element.35), channel_id=1, source_target_pairs={{0,4},{4,0},{8,12},{12,8},{1,5},{5,1},{9,13},{13,9},{2,6},{6,2},{1... | collective-permute-start | bytes 12296 | tf_op jit(solution)/shard_map/ppermute | solution.py:65
  11.5 5.8 %collective-permute-start.3 = (bf16[80,128]{1,0:T(8,128)(2,1)S(1)}, bf16[80,128]{1,0:T(8,128)(2,1)S(1)}, u32[]{:S(2)}, u32[]{:S(2)}) collective-permute-start(bf16[80,128]{1,0:T(8,128)(2,1)S(1)} %get-tuple-element.38), channel_id=1, source_target_pairs={{0,4},{4,0},{8,12},{12,8},{1,5},{5,1},{9,13},{13,9},{2,6},{6,2},{1... | collective-permute-start | bytes 61448 | tf_op jit(solution)/shard_map/ppermute | solution.py:49
  11.6 5.7 %collective-permute-start.4 = (bf16[80,128]{1,0:T(8,128)(2,1)S(1)}, bf16[80,128]{1,0:T(8,128)(2,1)S(1)}, u32[]{:S(2)}, u32[]{:S(2)}) collective-permute-start(bf16[80,128]{1,0:T(8,128)(2,1)S(1)} %get-tuple-element.39), channel_id=1, source_target_pairs={{0,12},{4,8},{8,4},{12,0},{1,13},{5,9},{9,5},{13,1},{2,14},{6,10},... | collective-permute-start | bytes 61448 | tf_op jit(solution)/shard_map/ppermute | solution.py:49
  17.5 3.1 %collective-permute-start.5 = (bf16[48,128]{1,0:T(8,128)(2,1)S(1)}, bf16[48,128]{1,0:T(8,128)(2,1)S(1)}, u32[]{:S(2)}, u32[]{:S(2)}) collective-permute-start(bf16[48,128]{1,0:T(8,128)(2,1)S(1)} %shard_map.138), channel_id=1, source_target_pairs={{0,1},{1,0},{2,3},{3,2},{4,5},{5,4},{6,7},{7,6},{8,9},{9,8},{10,11... | collective-permute-start | bytes 36872 | tf_op jit(solution)/shard_map/ppermute | solution.py:49
  17.5 3.2 %collective-permute-start.6 = (bf16[48,128]{1,0:T(8,128)(2,1)S(1)}, bf16[48,128]{1,0:T(8,128)(2,1)S(1)}, u32[]{:S(2)}, u32[]{:S(2)}) collective-permute-start(bf16[48,128]{1,0:T(8,128)(2,1)S(1)} %shard_map.138), channel_id=1, source_target_pairs={{0,3},{1,2},{2,1},{3,0},{4,7},{5,6},{6,5},{7,4},{8,11},{9,10},{10,... | collective-permute-start | bytes 36872 | tf_op jit(solution)/shard_map/ppermute | solution.py:49
  22.6 4.6 %collective-permute-start.7 = (f32[16,128]{1,0:T(8,128)S(1)}, f32[16,128]{1,0:T(8,128)S(1)}, u32[]{:S(2)}, u32[]{:S(2)}) collective-permute-start(f32[16,128]{1,0:T(8,128)S(1)} %get-tuple-element.53), channel_id=1, source_target_pairs={{0,8},{4,12},{8,0},{12,4},{1,9},{5,13},{9,1},{13,5},{2,10},{6,14},... | collective-permute-start | bytes 24584 | tf_op jit(solution)/shard_map/ppermute | solution.py:65
  23.4 5.5 %collective-permute-start.8 = (f32[16,128]{1,0:T(8,128)S(1)}, f32[16,128]{1,0:T(8,128)S(1)}, u32[]{:S(2)}, u32[]{:S(2)}) collective-permute-start(f32[16,128]{1,0:T(8,128)S(1)} %get-tuple-element.54), channel_id=1, source_target_pairs={{0,12},{4,8},{8,4},{12,0},{1,13},{5,9},{9,5},{13,1},{2,14},{6,10},... | collective-permute-start | bytes 24584 | tf_op jit(solution)/shard_map/ppermute | solution.py:65
  25.4 3.7 %collective-permute-start.9 = (f32[16,128]{1,0:T(8,128)S(1)}, f32[16,128]{1,0:T(8,128)S(1)}, u32[]{:S(2)}, u32[]{:S(2)}) collective-permute-start(f32[16,128]{1,0:T(8,128)S(1)} %get-tuple-element.55), channel_id=1, source_target_pairs={{0,4},{4,0},{8,12},{12,8},{1,5},{5,1},{9,13},{13,9},{2,6},{6,2},{1... | collective-permute-start | bytes 24584 | tf_op jit(solution)/shard_map/ppermute | solution.py:65
